TPU v7x, 32 devices: a whole 2x2x4 slice. The times are simulated.
32 devices in a mesh: page: 32 (over z, y, x, core), head: 1.
Axes of the slice: x: 2, y: 2, z: 4, core: 2. Of those that a mesh axis runs over, the one named last changes fastest.
Arguments:
- hidden: bfloat16 [12288, 4096], P('page'), may hold values from -6 to 6
- attention_norm_gain: bfloat16 [4096], replicated, may hold values from 0.25 to 1.75
- wq: bfloat16 [4096, 4096], P('page', 'head'), may hold values from -0.09375 to 0.09375
- adapter_down_weight: bfloat16 [4096, 512], P('head', 'page'), may hold values from -0.09375 to 0.09375
- adapter_up_weight: bfloat16 [512, 4096], P('page', 'head'), may hold values from -0.75 to 0.75
- key_value_cache: bfloat16 [12288, 2, 1024], P('page', None, 'head'), may hold values from -110 to 110
- logical_page_table: int32 [32, 3], P('page'), may hold values from 0 to 2, each once within a row
- lengths: int32 [8], replicated, may hold values from 1 to 3072, 12288 in all
- prompt_adapter_index: int32 [8], replicated, may hold values from 0 to 31
Outputs:
- queries: bfloat16 [12288, 4096], P('page', 'head')
- attended: bfloat16 [12288, 4096], P('page', 'head')
Inputs may be any that keep to these rules, and one draw needn't show every extreme that they name: The lengths sum to 12288 and the longest is exactly 3072. `logical_page_table`: each row is a permutation of the page slots of one index of page.
All inputs are finite; a program needn't handle non-finite values.
Results may differ from a plain program's by a relative error of at most 0.012.
The roundings to bfloat16 on the way count: a program that leaves them out, or rounds other values in their place, can miss the bound.
Values may be sent and summed in bfloat16 or wider, within the bound.
No kernel may reach another device: no remote copies, remote signals or barrier semaphores. Data moves between devices by JAX's collectives and lax.ppermute only.
A program may use at most 320 MiB of HBM per device.

v0:
```python
import math

import jax
import jax.numpy as jnp
from jax import lax
from jax.sharding import PartitionSpec as P

HEAD_WIDTH = 128
ADAPTER_RANK = 16


EPSILON = 1e-05
ROPE_BASE = 500000.0


def from_behind(value, axis, steps):
    count = lax.axis_size(axis)
    leading, last = (max(0, -steps), min(count, count - steps))
    return lax.ppermute(value, axis, [(source, source + steps) for source in range(leading, last)])


def apply_rotation(values_f, token_position, head_size):
    half = head_size // 2
    inverse = ROPE_BASE ** (-(jnp.arange(half, dtype=jnp.float32) * 2.0 / head_size))
    angle = token_position.astype(jnp.float32)[:, None] * inverse[None, :]
    cosine = jnp.cos(angle)[:, None, :]
    sine = jnp.sin(angle)[:, None, :]
    first = values_f[..., :half]
    second = values_f[..., half:]
    return jnp.concatenate(
        [first * cosine - second * sine, second * cosine + first * sine], axis=-1
    )


def score_block(query, keyblock):
    return lax.dot_general(
        query, keyblock, (((1,), (1,)), ((), ())), preferred_element_type=jnp.float32
    )


def mix_block(weights, valueblock):
    return jnp.dot(weights, valueblock, preferred_element_type=jnp.float32)


def normalize(scores, visible, inv_scale):
    scores = jnp.where(visible, scores * inv_scale, -jnp.inf)
    top = jnp.max(scores, axis=-1, keepdims=True)
    expo = jnp.exp(scores - top)
    return (expo / jnp.sum(expo, axis=-1, keepdims=True)).astype(jnp.bfloat16)


def body(
    hidden,
    attention_norm_gain,
    wq,
    adapter_down_weight,
    adapter_up_weight,
    key_value_cache,
    logical_page_table,
    lengths,
    prompt_adapter_index,
):
    token_device_rows = hidden.shape[0]
    page_index = lax.axis_index("page")
    head_index = lax.axis_index("head")
    span_count = lax.axis_size("page") // 4
    x = hidden.astype(jnp.float32)
    scale_rows = lax.rsqrt(jnp.mean(x * x, axis=-1, keepdims=True) + EPSILON)
    normed_input = (x * scale_rows * attention_norm_gain.astype(jnp.float32)).astype(jnp.bfloat16)
    ends = jnp.cumsum(lengths)
    starts = ends - lengths
    token = page_index * token_device_rows + jnp.arange(token_device_rows, dtype=jnp.int32)
    member = (token[:, None] >= starts[None, :]) & (token[:, None] < ends[None, :])
    tok_start = jnp.sum(jnp.where(member, starts[None, :], 0), axis=1)
    tok_adapter = jnp.sum(jnp.where(member, prompt_adapter_index[None, :], 0), axis=1)
    token_position = token - tok_start
    q_cols = wq.shape[1]
    base_query = jnp.dot(
        normed_input,
        lax.all_gather(wq, "page", axis=0, tiled=True),
        preferred_element_type=jnp.float32,
    )
    shrink_all, expand_every_token = (
        lax.all_gather(adapter_down_weight, "page", axis=1, tiled=True),
        lax.all_gather(adapter_up_weight, "page", axis=0, tiled=True),
    )
    adapter_count = shrink_all.shape[1] // ADAPTER_RANK
    feature_number = adapter_down_weight.shape[0]
    own_features = lax.dynamic_slice_in_dim(
        normed_input, head_index * feature_number, feature_number, 1
    )
    partial_every_token = jnp.dot(own_features, shrink_all, preferred_element_type=jnp.float32)
    partial_every_token = partial_every_token.reshape(
        token_device_rows, adapter_count, ADAPTER_RANK
    )
    pick = tok_adapter[:, None] == jnp.arange(adapter_count, dtype=jnp.int32)[None, :]
    partial_sum = jnp.sum(jnp.where(pick[:, :, None], partial_every_token, 0.0), axis=1)
    shrunk = lax.psum(partial_sum, "head").astype(jnp.bfloat16)
    spread_heads = jnp.where(pick[:, :, None], shrunk[:, None, :], jnp.zeros((), jnp.bfloat16))
    spread_heads = spread_heads.reshape(token_device_rows, adapter_count * ADAPTER_RANK)
    adapter_delta = jnp.dot(spread_heads, expand_every_token, preferred_element_type=jnp.float32)
    local_head_count = q_cols // HEAD_WIDTH
    queries = apply_rotation(
        (base_query + adapter_delta).reshape(token_device_rows, local_head_count, HEAD_WIDTH),
        token_position,
        HEAD_WIDTH,
    ).astype(jnp.bfloat16)
    kv_width = key_value_cache.shape[2]
    kv_heads = kv_width // HEAD_WIDTH
    page_count = logical_page_table.shape[1]
    paged = key_value_cache.reshape(page_count, token_device_rows // page_count, 2, kv_width)
    own_block = jnp.take(paged, logical_page_table[0], axis=0).reshape(
        token_device_rows, 2, kv_width
    )

    def pass_on(moving, unused):
        moved = from_behind(moving, "page", 1)
        return (moved, moved)

    unused_last, earlier = lax.scan(pass_on, own_block, None, length=span_count)
    stacked = jnp.concatenate([earlier[::-1], own_block[None]], axis=0)
    block_count = span_count + 1
    key_total = block_count * token_device_rows
    key_index = (page_index - span_count) * token_device_rows + jnp.arange(
        key_total, dtype=jnp.int32
    )
    visible = (key_index[None, :] >= tok_start[:, None]) & (key_index[None, :] <= token[:, None])
    inv_scale = 1.0 / math.sqrt(HEAD_WIDTH)
    group = local_head_count // kv_heads
    outputs = []
    for kv_head in range(kv_heads):
        low = kv_head * HEAD_WIDTH
        key_stack = stacked[:, :, 0, low : low + HEAD_WIDTH]
        value_stack = stacked[:, :, 1, low : low + HEAD_WIDTH]
        for member_head in range(group):
            query = queries[:, kv_head * group + member_head]
            keys_joined = key_stack.reshape(key_total, HEAD_WIDTH)
            values_joined = value_stack.reshape(key_total, HEAD_WIDTH)
            weights = normalize(score_block(query, keys_joined), visible, inv_scale)
            outputs.append(mix_block(weights, values_joined))
    attended = jnp.stack(outputs, axis=1).reshape(token_device_rows, q_cols).astype(jnp.bfloat16)
    return (queries.reshape(token_device_rows, q_cols), attended)


def solution(mesh):
    return jax.shard_map(
        body,
        mesh=mesh,
        in_specs=(
            P("page", None),
            P(),
            P("page", "head"),
            P("head", "page"),
            P("page", "head"),
            P("page", None, "head"),
            P("page", None),
            P(),
            P(),
        ),
        out_specs=(P("page", "head"), P("page", "head")),
        check_vma=False,
    )
```

profile of v0, /device:TPU:16, one launch (start us, length us, event | category | flops | bytes accessed | tf_op | source)
XLA Modules:
  0.0 711.1 jit_solution(5922468402307520090)
XLA Ops:
  18.1 382.6 %while.12 = (s32[]{:T(128)}, bf16[384,2,1024]{2,1,0:T(2,128)(2,1)}, bf16[8,384,2,1024]{3,1,0,2:T(8,128)(2,1)}, s32[]{:T(128)}) while((s32[]{:T(128)}, bf16[384,2,1024]{2,1,0:T(2,128)(2,1)}, bf16[8,384,2,1024]{3,1,0,2:T(8,128)(2,1)}, s32[]{:T(128)}) %tuple.78), condition=%wide.region_6.7_spmd, body=%wide.region_5.6_spmd.sunk | while | flops 2 | bytes 12583017 | solution.py:120
  20.3 27.7 %collective-permute-done = bf16[384,2,1024]{2,1,0:T(2,128)(2,1)S(1)} collective-permute-done((bf16[384,2,1024]{2,1,0:T(2,128)(2,1)}, bf16[384,2,1024]{2,1,0:T(2,128)(2,1)S(1)}, u32[]{:S(2)}, u32[]{:S(2)}) %collective-permute-start) | collective-permute-done | bytes 1572896 | tf_op jit(solution)/shard_map/while/body/eval_jaxpr/ppermute | solution.py:19
  52.7 33.1 %collective-permute-done = bf16[384,2,1024]{2,1,0:T(2,128)(2,1)S(1)} collective-permute-done((bf16[384,2,1024]{2,1,0:T(2,128)(2,1)}, bf16[384,2,1024]{2,1,0:T(2,128)(2,1)S(1)}, u32[]{:S(2)}, u32[]{:S(2)}) %collective-permute-start) | collective-permute-done | bytes 1572896 | tf_op jit(solution)/shard_map/while/body/eval_jaxpr/ppermute | solution.py:19
  90.5 44.3 %collective-permute-done = bf16[384,2,1024]{2,1,0:T(2,128)(2,1)S(1)} collective-permute-done((bf16[384,2,1024]{2,1,0:T(2,128)(2,1)}, bf16[384,2,1024]{2,1,0:T(2,128)(2,1)S(1)}, u32[]{:S(2)}, u32[]{:S(2)}) %collective-permute-start) | collective-permute-done | bytes 1572896 | tf_op jit(solution)/shard_map/while/body/eval_jaxpr/ppermute | solution.py:19
  139.5 57.8 %collective-permute-done = bf16[384,2,1024]{2,1,0:T(2,128)(2,1)S(1)} collective-permute-done((bf16[384,2,1024]{2,1,0:T(2,128)(2,1)}, bf16[384,2,1024]{2,1,0:T(2,128)(2,1)S(1)}, u32[]{:S(2)}, u32[]{:S(2)}) %collective-permute-start) | collective-permute-done | bytes 1572896 | tf_op jit(solution)/shard_map/while/body/eval_jaxpr/ppermute | solution.py:19
  202.0 74.6 %collective-permute-done = bf16[384,2,1024]{2,1,0:T(2,128)(2,1)S(1)} collective-permute-done((bf16[384,2,1024]{2,1,0:T(2,128)(2,1)}, bf16[384,2,1024]{2,1,0:T(2,128)(2,1)S(1)}, u32[]{:S(2)}, u32[]{:S(2)}) %collective-permute-start) | collective-permute-done | bytes 1572896 | tf_op jit(solution)/shard_map/while/body/eval_jaxpr/ppermute | solution.py:19
  281.3 48.2 %collective-permute-done = bf16[384,2,1024]{2,1,0:T(2,128)(2,1)S(1)} collective-permute-done((bf16[384,2,1024]{2,1,0:T(2,128)(2,1)}, bf16[384,2,1024]{2,1,0:T(2,128)(2,1)S(1)}, u32[]{:S(2)}, u32[]{:S(2)}) %collective-permute-start) | collective-permute-done | bytes 1572896 | tf_op jit(solution)/shard_map/while/body/eval_jaxpr/ppermute | solution.py:19
  334.1 24.6 %collective-permute-done = bf16[384,2,1024]{2,1,0:T(2,128)(2,1)S(1)} collective-permute-done((bf16[384,2,1024]{2,1,0:T(2,128)(2,1)}, bf16[384,2,1024]{2,1,0:T(2,128)(2,1)S(1)}, u32[]{:S(2)}, u32[]{:S(2)}) %collective-permute-start) | collective-permute-done | bytes 1572896 | tf_op jit(solution)/shard_map/while/body/eval_jaxpr/ppermute | solution.py:19
  363.4 34.6 %collective-permute-done = bf16[384,2,1024]{2,1,0:T(2,128)(2,1)S(1)} collective-permute-done((bf16[384,2,1024]{2,1,0:T(2,128)(2,1)}, bf16[384,2,1024]{2,1,0:T(2,128)(2,1)S(1)}, u32[]{:S(2)}, u32[]{:S(2)}) %collective-permute-start) | collective-permute-done | bytes 1572896 | tf_op jit(solution)/shard_map/while/body/eval_jaxpr/ppermute | solution.py:19
  400.7 10.5 %rev.3 = bf16[8,384,2,1024]{3,1,0,2:T(8,128)(2,1)} reverse(bf16[8,384,2,1024]{3,1,0,2:T(8,128)(2,1)} %get-tuple-element.19), dimensions={0} | reverse | bytes 25165824 | tf_op jit(solution)/shard_map/rev | solution.py:121
  416.0 5.9 pad_maximum_fusion
  424.4 4.4 fusion.199
  428.8 4.6 fusion.195
  433.7 20.1 %fusion.197 = f32[384,4096]{1,0:T(8,128)} fusion(bf16[4096,4096]{1,0:T(8,128)(2,1)} %all-gather.4.cloned.1.call-done, bf16[384,4096]{1,0:T(8,128)(2,1)S(1)} %copy-done, f32[4096]{0:T(1024)} %copy-done.19, f32[384]{0:T(512)} %copy-done.41), kind=kOutput, calls=%fused_computation.333 | convolution fusion | flops 12891193344 | bytes 43009536 | tf_op jit(solution)/shard_map/dot_general | solution.py:78
  453.8 8.5 %convolution_add_fusion = f32[384,4096]{1,0:T(8,128)} fusion(f32[384,4096]{1,0:T(8,128)} %fusion.197, bf16[384,512]{0,1:T(8,128)(2,1)S(1)} %bitcast.500, bf16[512,4096]{1,0:T(8,128)(2,1)} %all-gather.8.cloned.1.call-done), kind=kOutput, calls=%fused_computation.87 | convolution fusion | flops 1612185600 | bytes 17170432 | tf_op jit(solution)/shard_map/dot_general | solution.py:101
  462.3 7.1 %copy.147 = f32[384,4096]{0,1:T(8,128)} copy(f32[384,4096]{1,0:T(8,128)} %convolution_add_fusion) | data formatting | bytes 12582912 | tf_op jit(solution)/shard_map/reshape | solution.py:104
  469.5 3.8 multiply_subtract_fusion
  474.5 3.9 fusion.215
  478.4 3.8 fusion.216
  482.2 3.9 fusion.217
  486.1 3.9 fusion.218
  490.1 3.9 fusion.219
  493.9 3.9 fusion.220
  497.8 4.1 fusion.221
  501.9 3.9 fusion.222
  505.8 3.9 fusion.223
  509.6 3.9 fusion.224
  513.6 4.0 fusion.225
  521.4 3.9 fusion.227
  529.1 4.6 fusion.229
  533.8 4.5 fusion.230
  538.3 4.4 fusion.231
  542.7 4.6 fusion.232
  547.2 4.4 fusion.233
  551.7 4.5 fusion.234
  556.2 4.4 fusion.235
  560.6 4.9 fusion.236
  565.5 4.5 fusion.237
  570.0 4.5 fusion.238
  574.5 4.5 fusion.239
  579.1 4.4 fusion.240
  583.5 4.5 fusion.241
  588.0 4.4 fusion.242
  592.5 4.5 fusion.243
  597.0 4.6 fusion.244
  601.5 4.5 fusion.245
  606.0 4.5 fusion.246
  616.9 3.9 fusion.132
  (376 shorter events, 153.2 us)
Async XLA Ops:
  7.2 421.6 %all-gather.6.cloned.1.call-start = ((), (), s32[]{:S(2)}) async-start(), calls=%async_computation.1 | async-start | bytes 4325376 | tf_op jit(solution)/shard_map/all_gather | solution.py:84
  7.9 425.8 %all-gather.4.cloned.1.call-start = ((), (), s32[]{:S(2)}) async-start(), calls=%async_computation | async-start | bytes 34603008 | tf_op jit(solution)/shard_map/all_gather | solution.py:80
  8.6 445.1 %all-gather.8.cloned.1.call-start = ((), (), s32[]{:S(2)}) async-start(), calls=%async_computation.2 | async-start | bytes 4325376 | tf_op jit(solution)/shard_map/all_gather | solution.py:85
  11.4 417.4 %copy-start.19 = (f32[4096]{0:T(1024)}, f32[4096]{0:T(1024)S(1)}, u32[]{:S(2)}) copy-start(f32[4096]{0:T(1024)S(1)} %convert_element_type.131) | copy-start | bytes 49156
  18.4 29.6 %collective-permute-start = (bf16[384,2,1024]{2,1,0:T(2,128)(2,1)}, bf16[384,2,1024]{2,1,0:T(2,128)(2,1)S(1)}, u32[]{:S(2)}, u32[]{:S(2)}) collective-permute-start(bf16[384,2,1024]{2,1,0:T(2,128)(2,1)} %get-tuple-element.152), channel_id=1, source_target_pairs={{0,1},{1,2},{2,3},{3,4},{4,5},{5,6},{6,7},{7,8},{8,9},{9,10},{10,1... | collective-permute-start | bytes 4718600 | tf_op jit(solution)/shard_map/while/body/eval_jaxpr/ppermute | solution.py:19
  50.8 35.1 %collective-permute-start = (bf16[384,2,1024]{2,1,0:T(2,128)(2,1)}, bf16[384,2,1024]{2,1,0:T(2,128)(2,1)S(1)}, u32[]{:S(2)}, u32[]{:S(2)}) collective-permute-start(bf16[384,2,1024]{2,1,0:T(2,128)(2,1)} %get-tuple-element.152), channel_id=1, source_target_pairs={{0,1},{1,2},{2,3},{3,4},{4,5},{5,6},{6,7},{7,8},{8,9},{9,10},{10,1... | collective-permute-start | bytes 4718600 | tf_op jit(solution)/shard_map/while/body/eval_jaxpr/ppermute | solution.py:19
  88.6 46.2 %collective-permute-start = (bf16[384,2,1024]{2,1,0:T(2,128)(2,1)}, bf16[384,2,1024]{2,1,0:T(2,128)(2,1)S(1)}, u32[]{:S(2)}, u32[]{:S(2)}) collective-permute-start(bf16[384,2,1024]{2,1,0:T(2,128)(2,1)} %get-tuple-element.152), channel_id=1, source_target_pairs={{0,1},{1,2},{2,3},{3,4},{4,5},{5,6},{6,7},{7,8},{8,9},{9,10},{10,1... | collective-permute-start | bytes 4718600 | tf_op jit(solution)/shard_map/while/body/eval_jaxpr/ppermute | solution.py:19
  137.5 59.8 %collective-permute-start = (bf16[384,2,1024]{2,1,0:T(2,128)(2,1)}, bf16[384,2,1024]{2,1,0:T(2,128)(2,1)S(1)}, u32[]{:S(2)}, u32[]{:S(2)}) collective-permute-start(bf16[384,2,1024]{2,1,0:T(2,128)(2,1)} %get-tuple-element.152), channel_id=1, source_target_pairs={{0,1},{1,2},{2,3},{3,4},{4,5},{5,6},{6,7},{7,8},{8,9},{9,10},{10,1... | collective-permute-start | bytes 4718600 | tf_op jit(solution)/shard_map/while/body/eval_jaxpr/ppermute | solution.py:19
  200.1 76.6 %collective-permute-start = (bf16[384,2,1024]{2,1,0:T(2,128)(2,1)}, bf16[384,2,1024]{2,1,0:T(2,128)(2,1)S(1)}, u32[]{:S(2)}, u32[]{:S(2)}) collective-permute-start(bf16[384,2,1024]{2,1,0:T(2,128)(2,1)} %get-tuple-element.152), channel_id=1, source_target_pairs={{0,1},{1,2},{2,3},{3,4},{4,5},{5,6},{6,7},{7,8},{8,9},{9,10},{10,1... | collective-permute-start | bytes 4718600 | tf_op jit(solution)/shard_map/while/body/eval_jaxpr/ppermute | solution.py:19
  279.3 50.1 %collective-permute-start = (bf16[384,2,1024]{2,1,0:T(2,128)(2,1)}, bf16[384,2,1024]{2,1,0:T(2,128)(2,1)S(1)}, u32[]{:S(2)}, u32[]{:S(2)}) collective-permute-start(bf16[384,2,1024]{2,1,0:T(2,128)(2,1)} %get-tuple-element.152), channel_id=1, source_target_pairs={{0,1},{1,2},{2,3},{3,4},{4,5},{5,6},{6,7},{7,8},{8,9},{9,10},{10,1... | collective-permute-start | bytes 4718600 | tf_op jit(solution)/shard_map/while/body/eval_jaxpr/ppermute | solution.py:19
  332.2 26.5 %collective-permute-start = (bf16[384,2,1024]{2,1,0:T(2,128)(2,1)}, bf16[384,2,1024]{2,1,0:T(2,128)(2,1)S(1)}, u32[]{:S(2)}, u32[]{:S(2)}) collective-permute-start(bf16[384,2,1024]{2,1,0:T(2,128)(2,1)} %get-tuple-element.152), channel_id=1, source_target_pairs={{0,1},{1,2},{2,3},{3,4},{4,5},{5,6},{6,7},{7,8},{8,9},{9,10},{10,1... | collective-permute-start | bytes 4718600 | tf_op jit(solution)/shard_map/while/body/eval_jaxpr/ppermute | solution.py:19
  361.4 36.5 %collective-permute-start = (bf16[384,2,1024]{2,1,0:T(2,128)(2,1)}, bf16[384,2,1024]{2,1,0:T(2,128)(2,1)S(1)}, u32[]{:S(2)}, u32[]{:S(2)}) collective-permute-start(bf16[384,2,1024]{2,1,0:T(2,128)(2,1)} %get-tuple-element.152), channel_id=1, source_target_pairs={{0,1},{1,2},{2,3},{3,4},{4,5},{5,6},{6,7},{7,8},{8,9},{9,10},{10,1... | collective-permute-start | bytes 4718600 | tf_op jit(solution)/shard_map/while/body/eval_jaxpr/ppermute | solution.py:19
  400.7 11.1 %copy-start.43 = (s32[8]{0:T(128)S(1)}, s32[8]{0:T(128)}, u32[]{:S(2)}) copy-start(s32[8]{0:T(128)} %param.18) | copy-start | bytes 100
  400.7 11.1 %copy-start.42 = (s32[8]{0:T(128)S(1)}, s32[8]{0:T(128)}, u32[]{:S(2)}) copy-start(s32[8]{0:T(128)} %param.19) | copy-start | bytes 100
  411.9 9.9 %copy-start.21 = (s32[384]{0:T(512)}, s32[384]{0:T(512)S(1)}, u32[]{:S(2)}) copy-start(s32[384]{0:T(512)S(1)} %get-tuple-element.36) | copy-start | bytes 4612
  414.5 14.2 %copy-start.41 = (f32[384]{0:T(512)}, f32[384]{0:T(512)S(1)}, u32[]{:S(2)}) copy-start(f32[384]{0:T(512)S(1)} %add_rsqrt_fusion) | copy-start | bytes 4612
  415.7 6.2 slice-start
  416.0 7.2 %slice-start.1 = ((s8[12582912]{0:T(1024)(128)(4,1)}), s8[4194304]{0:T(1024)(128)(4,1)S(1)}, s32[]{:S(2)}) async-start(s8[12582912]{0:T(1024)(128)(4,1)} %bitcast.430), calls=%async_computation.4 | async-start | bytes 8388608
  416.0 8.4 %slice-start.2 = ((s8[12582912]{0:T(1024)(128)(4,1)}), s8[4194304]{0:T(1024)(128)(4,1)S(1)}, s32[]{:S(2)}) async-start(s8[12582912]{0:T(1024)(128)(4,1)} %bitcast.430), calls=%async_computation.5 | async-start | bytes 8388608
  424.4 4.4 copy-start
  462.3 7.1 %copy-start.17 = (f32[384,64]{0,1:T(8,128)S(1)}, f32[384,64]{0,1:T(8,128)}, u32[]{:S(2)}) copy-start(f32[384,64]{0,1:T(8,128)} %get-tuple-element.62) | copy-start | bytes 294916
  462.3 7.1 %copy-start.18 = (f32[384,64]{0,1:T(8,128)S(1)}, f32[384,64]{0,1:T(8,128)}, u32[]{:S(2)}) copy-start(f32[384,64]{0,1:T(8,128)} %get-tuple-element.63) | copy-start | bytes 294916
  486.1 4.0 copy-start.15
  501.9 3.9 copy-start.14
  517.5 3.8 copy-start.13
  533.8 4.5 copy-start.12
  551.7 4.5 copy-start.11
  570.0 4.5 copy-start.10
  588.0 4.4 copy-start.9
  613.4 3.5 copy-start.8
  613.4 7.4 %slice-start.63 = ((s8[5308416]{0:T(1024)(128)(4,1)}), s8[4194304]{0:T(1024)(128)(4,1)S(1)}, s32[]{:S(2)}) async-start(s8[5308416]{0:T(1024)(128)(4,1)} %bitcast.496), calls=%async_computation.66 | async-start | bytes 8388608
  616.9 3.9 slice-start.64
  626.3 4.8 slice-start.55
  627.1 3.9 slice-start.56
  637.7 4.8 slice-start.47
  638.6 3.9 slice-start.48
  648.9 4.8 slice-start.39
  649.8 3.9 slice-start.40
  655.9 3.6 slice-start.35
  658.2 3.6 slice-start.33
  659.6 3.1 slice-start.31
  664.9 3.8 slice-start.27
  668.7 4.8 slice-start.23
  669.6 3.9 slice-start.24
  678.1 4.5 slice-start.17
  679.9 3.5 slice-start.15
  688.0 4.1 slice-start.9
  689.8 3.1 slice-start.7
  (72 other events, 142.6 us)
Sparse Core Ops, SparseCore 0:
  10.9 69.8 all-gather.5
  83.6 239.1 all-gather.3
  325.7 71.5 all-gather.7
where the time goes:
time: 715 us; the launch traced here: 711 us
  waiting for transfers between devices  347 us (49%)
  matrix products  215 us (30%)
  local copies, waits for them, and re-layouts  65.4 us (9%)
  other arithmetic  52.4 us (7%)
  starting transfers between devices  15.4 us (2%)
  between operations  15.4 us (2%)
    ppermute x8, waiting for transfers between devices, from_behind(): lax.ppermute(value, axis, [(source, source + steps) for source in range(l...  345 us
    dot_general x32, matrix products, score_block(): lax.dot_general(query, keyblock, (((1,), (1,)), ((), ())), preferred_elem...  136 us
    dot_general x32, matrix products, mix_block(): return jnp.dot(weights, valueblock, preferred_element_type=jnp.float32)  45.8 us
    reduce_sum x32, other arithmetic, normalize(): return (expo / jnp.sum(expo, axis=-1, keepdims=True)).astype(jnp.bfloat16)  29.8 us
    unnamed x220, local copies, waits for them, and re-layouts  20.3 us
    dot_general x1, matrix products, body(): jnp.dot(normed_input, lax.all_gather(wq, 'page', axis=0, tiled=True), pre...  20.1 us
    ppermute x8, starting transfers between devices, from_behind(): lax.ppermute(value, axis, [(source, source + steps) for source in range(l...  15.3 us
  transfers between devices with their start and end apart: 11, of which 8 were waited for; matrix products, arithmetic and copies ran while one was open for 11% of the time, Pallas kernels for 0%

commit v1 on v0

--- a/solution.py
+++ b/solution.py
@@ -1,8 +1,11 @@
+import functools
 import math
 
 import jax
 import jax.numpy as jnp
 from jax import lax
+from jax.experimental import pallas as pl
+from jax.experimental.pallas import tpu as pltpu
 from jax.sharding import PartitionSpec as P
 
 HEAD_WIDTH = 128
@@ -11,6 +14,8 @@
 
 EPSILON = 1e-05
 ROPE_BASE = 500000.0
+KEY_TILE = 512
+LOWEST = -1e30
 
 
 def from_behind(value, axis, steps):
@@ -142,9 +147,674 @@
     return (queries.reshape(token_device_rows, q_cols), attended)
 
 
+PAIR = 4
+
+
+def swap(value, bit):
+    count = lax.axis_size("page")
+    return lax.ppermute(value, "page", [(p, p ^ bit) for p in range(count)])
+
+
+def shift_z(value, steps):
+    count = lax.axis_size("page")
+    return lax.ppermute(value, "page", [(p, (p + 8 * steps) % count) for p in range(count)])
+
+
+class Transfers:
+    def __init__(self):
+        self.found = {}
+
+    def __getitem__(self, name):
+        return self.found[name]
+
+    def tie(self, values, waits):
+        waits = list(waits)
+        tied = lax.optimization_barrier((*values, *[self.found[name] for name in waits]))
+        for name, value in zip(waits, tied[len(values) :]):
+            self.found[name] = value
+        return list(tied[: len(values)])
+
+    def run(self, waits, sends):
+        operands = [operand for _, operand, _ in sends]
+        if waits:
+            operands = self.tie(operands, waits)
+        for (name, _, move), operand in zip(sends, operands):
+            self.found[name] = move(operand)
+
+
+def in_order(flag, one, other):
+    return jnp.where(
+        flag == 0,
+        jnp.concatenate([one, other], axis=0),
+        jnp.concatenate([other, one], axis=0),
+    )
+
+
+def member_rows(value, first_token, starts, ends):
+    token = first_token + lax.broadcasted_iota(jnp.int32, (1, value.shape[1]), 1)
+    return [
+        jnp.where((token >= start) & (token < end), value, 0.0) for start, end in zip(starts, ends)
+    ]
+
+
+def choose_kernel(which, every_ref, out_ref, held, sems):
+    slots = which.shape[0]
+    rank = every_ref.shape[1] // 2
+    copies = []
+    for r in range(slots):
+        for kind in range(2):
+            copies.append(
+                pltpu.make_async_copy(
+                    every_ref.at[which[r], pl.ds(kind * rank, rank)],
+                    held.at[pl.ds((kind * slots + r) * rank, rank)],
+                    sems.at[kind, r],
+                )
+            )
+    for copy in copies:
+        copy.start()
+    for copy in copies:
+        copy.wait()
+    rows, width = out_ref.shape
+    part = held.shape[1]
+    for h in range(width // part):
+        out_ref[:, h * part : (h + 1) * part] = held[h * rows : (h + 1) * rows]
+
+
+def choose(which, every, width):
+    slots = which.shape[0]
+    _, rows, part = every.shape
+    return pl.pallas_call(
+        choose_kernel,
+        out_shape=jax.ShapeDtypeStruct((slots * rows * part // width, width), every.dtype),
+        in_specs=[pl.BlockSpec(memory_space=pltpu.SMEM), pl.BlockSpec(memory_space=pl.ANY)],
+        out_specs=pl.BlockSpec(memory_space=pltpu.VMEM),
+        scratch_shapes=[
+            pltpu.VMEM((slots * rows, part), every.dtype),
+            pltpu.SemaphoreType.DMA((2, slots)),
+        ],
+        cost_estimate=pl.CostEstimate(flops=1000, bytes_accessed=1000, transcendentals=0),
+        name="choose",
+    )(which, every)
+
+
+def shrink_kernel(layout, blocks, depth, part, numbers, *refs):
+    normed_refs, refs = refs[: len(layout)], refs[len(layout) :]
+    weight_refs, refs = refs[:blocks], refs[blocks:]
+    out_ref, up_ref, held, adapters, normed_sems, sems = refs
+    rank, columns = out_ref.shape
+    rows = columns // PAIR
+    features = held.shape[2]
+    slots = adapters.shape[0] // (2 * rank)
+    extra = weight_refs[0].shape[0] - depth
+    quarter = numbers[0]
+    columns_here = pl.ds(pl.multiple_of(quarter * features, features), features)
+    copies = [
+        pltpu.make_async_copy(
+            ref.at[:, columns_here], held.at[i, pl.ds(low, ref.shape[0])], normed_sems.at[n]
+        )
+        for n, (ref, (i, low)) in enumerate(zip(normed_refs, layout))
+    ]
+    for b in range(blocks):
+        place = pl.multiple_of(numbers[1 + b] * part, part)
+        for h in range(2 * slots * rank // extra):
+            copies.append(
+                pltpu.make_async_copy(
+                    weight_refs[b].at[pl.ds(depth, extra), pl.ds(h * part, part)],
+                    adapters.at[pl.ds(h * extra, extra), pl.ds(place, part)],
+                    sems.at[b, h],
+                )
+            )
+    for copy in copies:
+        copy.start()
+    for copy in copies:
+        copy.wait()
+    up_ref[...] = adapters[slots * rank :]
+    at = 1 + blocks + PAIR
+    starts = [numbers[at + r] for r in range(slots)]
+    ends = [numbers[at + slots + r] for r in range(slots)]
+    for i in range(PAIR):
+        partial = lax.dot_general(
+            adapters[: slots * rank],
+            held[i],
+            (((1,), (1,)), ((), ())),
+            preferred_element_type=jnp.float32,
+        )
+        token = numbers[1 + blocks + i] + lax.broadcasted_iota(jnp.int32, (1, rows), 1)
+        found = jnp.zeros((rank, rows), jnp.float32)
+        for r in range(slots):
+            member = (token >= starts[r]) & (token < ends[r])
+            found += jnp.where(member, partial[r * rank : (r + 1) * rank], 0.0)
+        place = pl.multiple_of((quarter ^ i) * rows, HEAD_WIDTH)
+        out_ref[:, pl.ds(place, rows)] = found
+
+
+def shrink(numbers, layout, normed, weights, depth, part, slots, rank):
+    rows, _ = normed[0].shape
+    blocks = len(weights)
+    extra, width = weights[0].shape[0] - depth, blocks * part
+    vmem = pl.BlockSpec(memory_space=pltpu.VMEM)
+    return pl.pallas_call(
+        functools.partial(shrink_kernel, layout, blocks, depth, part),
+        out_shape=(
+            jax.ShapeDtypeStruct((rank, PAIR * rows), jnp.float32),
+            jax.ShapeDtypeStruct((slots * rank, width), jnp.bfloat16),
+        ),
+        in_specs=[pl.BlockSpec(memory_space=pltpu.SMEM)]
+        + [pl.BlockSpec(memory_space=pl.ANY)] * (len(layout) + blocks),
+        out_specs=(vmem, vmem),
+        scratch_shapes=[
+            pltpu.VMEM((PAIR, rows, width), jnp.bfloat16),
+            pltpu.VMEM((2 * slots * rank, width), jnp.bfloat16),
+            pltpu.SemaphoreType.DMA((len(layout),)),
+            pltpu.SemaphoreType.DMA((blocks, 2 * slots * rank // extra)),
+        ],
+        compiler_params=pltpu.CompilerParams(vmem_limit_bytes=60 * 1024 * 1024),
+        cost_estimate=pl.CostEstimate(flops=1000, bytes_accessed=1000, transcendentals=0),
+        name="shrink",
+    )(numbers, *normed, *weights)
+
+
+def project_kernel(layout, blocks, numbers, *refs):
+    normed_refs, refs = refs[: len(layout)], refs[len(layout) :]
+    weight_refs, refs = refs[:blocks], refs[blocks:]
+    shrunk_ref, up_ref, cosine_ref, sine_ref, out_ref, held, weight, sems = refs
+    width = out_ref.shape[2]
+    rows = out_ref.shape[1]
+    depth = weight.shape[0] // blocks
+    rank = shrunk_ref.shape[0]
+    slots = up_ref.shape[0] // rank
+    weight_copies = [
+        pltpu.make_async_copy(
+            weight_refs[b].at[pl.ds(0, depth)],
+            weight.at[pl.ds(pl.multiple_of(numbers[1 + b] * depth, depth), depth)],
+            sems.at[len(layout) + b],
+        )
+        for b in range(blocks)
+    ]
+    copies = [
+        pltpu.make_async_copy(ref, held.at[i, pl.ds(low, ref.shape[0])], sems.at[n])
+        for n, (ref, (i, low)) in enumerate(zip(normed_refs, layout))
+    ]
+    for copy in weight_copies + copies:
+        copy.start()
+    for copy in weight_copies:
+        copy.wait()
+    at = 1 + blocks + PAIR
+    starts = [numbers[at + r] for r in range(slots)]
+    ends = [numbers[at + slots + r] for r in range(slots)]
+    for i in range(PAIR):
+        for copy, (block, _) in zip(copies, layout):
+            if block == i:
+                copy.wait()
+        block = numbers[0] ^ i
+        place = pl.multiple_of(block * rows, HEAD_WIDTH)
+        shrunk = shrunk_ref[:, pl.ds(place, rows)].astype(jnp.float32)
+        spread = member_rows(shrunk, numbers[1 + blocks + i], starts, ends)
+        spread = jnp.concatenate(spread, axis=0).astype(jnp.bfloat16)
+        total = lax.dot_general(
+            spread, up_ref[...], (((0,), (0,)), ((), ())), preferred_element_type=jnp.float32
+        )
+        total += jnp.dot(held[i], weight[...], preferred_element_type=jnp.float32)
+        cosine = cosine_ref[block]
+        sine = sine_ref[block]
+        for low in range(0, width, HEAD_WIDTH):
+            head = total[:, low : low + HEAD_WIDTH]
+            turned = head * cosine + pltpu.roll(head, HEAD_WIDTH // 2, 1) * sine
+            out_ref[block, :, low : low + HEAD_WIDTH] = turned.astype(jnp.bfloat16)
+
+
+def project(numbers, layout, normed, weights, shrunk, up, cosine, sine):
+    rows, features = normed[0].shape
+    width = weights[0].shape[1]
+    blocks = len(weights)
+    vmem = pl.BlockSpec(memory_space=pltpu.VMEM)
+    return pl.pallas_call(
+        functools.partial(project_kernel, layout, blocks),
+        out_shape=jax.ShapeDtypeStruct((PAIR, rows, width), jnp.bfloat16),
+        in_specs=[pl.BlockSpec(memory_space=pltpu.SMEM)]
+        + [pl.BlockSpec(memory_space=pl.ANY)] * (len(layout) + blocks)
+        + [vmem] * 4,
+        out_specs=vmem,
+        scratch_shapes=[
+            pltpu.VMEM((PAIR, rows, features), jnp.bfloat16),
+            pltpu.VMEM((features, width), jnp.bfloat16),
+            pltpu.SemaphoreType.DMA((len(layout) + blocks,)),
+        ],
+        compiler_params=pltpu.CompilerParams(vmem_limit_bytes=60 * 1024 * 1024),
+        cost_estimate=pl.CostEstimate(flops=1000, bytes_accessed=1000, transcendentals=0),
+        name="project",
+    )(numbers, *normed, *weights, shrunk, up, cosine, sine)
+
+
+def attend_kernel(
+    column,
+    numbers,
+    start_ref,
+    query_ref,
+    older_ref,
+    old_ref,
+    own_ref,
+    out_ref,
+    keys,
+    values,
+    turned,
+    total,
+    top_ref,
+    sems,
+):
+    step = pl.program_id(0)
+    tiles = pl.num_programs(0)
+    rows = own_ref.shape[0] // PAIR
+    tile_rows = query_ref.shape[1]
+    group = query_ref.shape[2] // HEAD_WIDTH
+    value_column = own_ref.shape[1] // 2 + column
+
+    @pl.when(step == 0)
+    def _():
+        copies = []
+        for kind, (low, target) in enumerate(((value_column, values), (column, keys))):
+            for b, source in enumerate((older_ref, old_ref, own_ref)):
+                for i in range(PAIR):
+                    place = pl.multiple_of(numbers[2 * tiles + i] + b * PAIR * rows, rows)
+                    copies.append(
+                        pltpu.make_async_copy(
+                            source.at[pl.ds(i * rows, rows), pl.ds(low, HEAD_WIDTH)],
+                            target.at[pl.ds(place, rows)],
+                            sems.at[kind, b * PAIR + i],
+                        )
+                    )
+        for copy in copies:
+            copy.start()
+        ones = turned.shape[0] - HEAD_WIDTH
+        turned[HEAD_WIDTH:] = jnp.ones((ones, turned.shape[1]), jnp.bfloat16)
+        for copy in copies[: len(copies) // 2]:
+            copy.wait()
+
+        def turn(i, carry):
+            low = pl.multiple_of(i * KEY_TILE, KEY_TILE)
+            turned[:HEAD_WIDTH, pl.ds(low, KEY_TILE)] = values[pl.ds(low, KEY_TILE)].T
+            return carry
+
+        lax.fori_loop(0, keys.shape[0] // KEY_TILE, turn, 0)
+        for copy in copies[len(copies) // 2 :]:
+            copy.wait()
+
+    first_token = numbers[step]
+    low_start = numbers[tiles + step]
+    base = numbers[2 * tiles + PAIR]
+    queries = [query_ref[0, :, h * HEAD_WIDTH : (h + 1) * HEAD_WIDTH] for h in range(group)]
+    factor = math.log2(math.e) / math.sqrt(HEAD_WIDTH)
+    top_ref[...] = jnp.full(top_ref.shape, LOWEST, jnp.float32)
+    total[...] = jnp.zeros(total.shape, jnp.float32)
+
+    def one_tile(tile, carry):
+        low = pl.multiple_of(tile * KEY_TILE, KEY_TILE)
+        shape = (KEY_TILE, tile_rows)
+        key_index = base + low + lax.broadcasted_iota(jnp.int32, shape, 0)
+        token = first_token + lax.broadcasted_iota(jnp.int32, shape, 1)
+        seen = (key_index <= token) & (key_index >= start_ref[0])
+        here = keys[pl.ds(low, KEY_TILE)]
+        products = [
+            lax.dot_general(
+                here, query, (((1,), (1,)), ((), ())), preferred_element_type=jnp.float32
+            )
+            for query in queries
+        ]
+        for h in range(group):
+            scores = jnp.where(seen, products[h] * factor, LOWEST)
+            old_top = top_ref[h]
+            new_top = jnp.maximum(old_top, jnp.max(scores, axis=0, keepdims=True))
+            expo = jnp.exp2(scores - new_top)
+            top_ref[h] = new_top
+            total[h] = total[h] * jnp.exp2(old_top - new_top) + jnp.dot(
+                turned[:, pl.ds(low, KEY_TILE)],
+                expo.astype(jnp.bfloat16),
+                preferred_element_type=jnp.float32,
+            )
+        return carry
+
+    from_tile = (low_start - base) // KEY_TILE
+    to_tile = (first_token + tile_rows - 1 - base) // KEY_TILE + 1
+    lax.fori_loop(from_tile, to_tile, one_tile, 0)
+    for h in range(group):
+        mixed = total[h, :HEAD_WIDTH] / total[h, HEAD_WIDTH : HEAD_WIDTH + 1]
+        out_ref[0, :, h * HEAD_WIDTH : (h + 1) * HEAD_WIDTH] = mixed.T.astype(jnp.bfloat16)
+
+
+def attend(column, numbers, tile_starts, queries, older, old, own):
+    tiles, tile_rows, width = queries.shape
+    key_total = 3 * own.shape[0]
+    group = width // HEAD_WIDTH
+    deep = HEAD_WIDTH + 16
+    anywhere = pl.BlockSpec(memory_space=pl.ANY)
+    return pl.pallas_call(
+        functools.partial(attend_kernel, column),
+        grid_spec=pltpu.PrefetchScalarGridSpec(
+            num_scalar_prefetch=1,
+            grid=(tiles,),
+            in_specs=[
+                pl.BlockSpec((1, 1, tile_rows), lambda i, n: (i, 0, 0)),
+                pl.BlockSpec((1, tile_rows, width), lambda i, n: (i, 0, 0)),
+                anywhere,
+                anywhere,
+                anywhere,
+            ],
+            out_specs=pl.BlockSpec((1, tile_rows, width), lambda i, n: (i, 0, 0)),
+            scratch_shapes=[
+                pltpu.VMEM((key_total, HEAD_WIDTH), jnp.bfloat16),
+                pltpu.VMEM((key_total, HEAD_WIDTH), jnp.bfloat16),
+                pltpu.VMEM((deep, key_total), jnp.bfloat16),
+                pltpu.VMEM((group, deep, tile_rows), jnp.float32),
+                pltpu.VMEM((group, 1, tile_rows), jnp.float32),
+                pltpu.SemaphoreType.DMA((2, 3 * PAIR)),
+            ],
+        ),
+        out_shape=jax.ShapeDtypeStruct(queries.shape, jnp.bfloat16),
+        compiler_params=pltpu.CompilerParams(vmem_limit_bytes=60 * 1024 * 1024),
+        cost_estimate=pl.CostEstimate(flops=1000, bytes_accessed=1000, transcendentals=0),
+        name="attend",
+    )(numbers, tile_starts, queries, older, old, own)
+
+
+def pair_body(
+    hidden,
+    attention_norm_gain,
+    wq,
+    adapter_down_weight,
+    adapter_up_weight,
+    key_value_cache,
+    logical_page_table,
+    lengths,
+    prompt_adapter_index,
+):
+    rows, features = hidden.shape
+    count = lax.axis_size("page")
+    me = lax.axis_index("page")
+    core, x, y, z = me % 2, (me // 2) % 2, (me // 4) % 2, me // 8
+    pair = me // PAIR
+    quarter = me % PAIR
+    q_cols = wq.shape[1]
+    width = q_cols // PAIR
+    kv_width = key_value_cache.shape[2]
+    kv_part = kv_width // PAIR
+    kv_heads = kv_part // HEAD_WIDTH
+    chunk = width // kv_heads
+
+    def weight_part(part_x, part_core):
+        return lax.dynamic_slice_in_dim(wq, (2 * part_x + part_core) * width, width, 1)
+
+    sent = Transfers()
+    core_swap = functools.partial(swap, bit=1)
+    x_swap = functools.partial(swap, bit=2)
+    y_swap = functools.partial(swap, bit=4)
+    wq_rows = wq.shape[0]
+    wq_depth = PAIR * wq_rows
+    pairs = count // PAIR
+    z_count = count // 8
+    order = (0, 1, 3, 2)
+
+    rank = adapter_up_weight.shape[0]
+    slots = prompt_adapter_index.shape[0]
+    part = width // pairs
+    both = jnp.concatenate([adapter_down_weight.T, adapter_up_weight], axis=0)
+    both = both.reshape(2 * rank, PAIR, pairs, part).transpose(2, 1, 0, 3)
+    both = both.reshape(count * 2 * rank, part)
+
+    def exchange(value):
+        return lax.all_to_all(value, "page", split_axis=0, concat_axis=0, tiled=True)
+
+    sent.run([], [("adapters", both, exchange)])
+    sent.run(
+        [],
+        [
+            (
+                "weight c",
+                jnp.concatenate([weight_part(x, 1 - core), weight_part(1 - x, 1 - core)], axis=0),
+                core_swap,
+            )
+        ],
+    )
+    from_core = sent["weight c"]
+    mine = in_order(core, weight_part(1 - x, core), from_core[wq_rows:])
+    kept = in_order(core, weight_part(x, core), from_core[:wq_rows])
+    sent.run([], [("weight x0", mine[:, :chunk], x_swap)])
+    key_value_cache, hidden = sent.tie([key_value_cache, hidden], ["weight x0"])
+
+    page_count = logical_page_table.shape[1]
+    page_rows = rows // page_count
+    paged = key_value_cache.reshape(page_count, page_rows, 2, kv_width)
+    ordered = jnp.concatenate(
+        [
+            lax.dynamic_index_in_dim(paged, logical_page_table[0, j], 0, keepdims=False)
+            for j in range(page_count)
+        ],
+        axis=0,
+    ).reshape(rows, 2 * kv_width)
+
+    def cache_part(part_x, part_core):
+        low = (2 * part_x + part_core) * kv_part
+        return jnp.concatenate(
+            [
+                lax.dynamic_slice_in_dim(ordered, low, kv_part, 1),
+                lax.dynamic_slice_in_dim(ordered, kv_width + low, kv_part, 1),
+            ],
+            axis=1,
+        )
+
+    sent.run(
+        [],
+        [
+            (
+                "cache c",
+                jnp.concatenate([cache_part(x, 1 - core), cache_part(1 - x, 1 - core)], axis=0),
+                core_swap,
+            )
+        ],
+    )
+    cache_core = sent["cache c"]
+
+    wide = hidden.astype(jnp.float32)
+    scale_rows = lax.rsqrt(jnp.mean(wide * wide, axis=-1, keepdims=True) + EPSILON)
+    normed_own = (wide * scale_rows * attention_norm_gain.astype(jnp.float32)).astype(jnp.bfloat16)
+    half_rows = rows // 2
+    ends = jnp.cumsum(lengths)
+    starts = ends - lengths
+    first_token = pair * (PAIR * rows)
+    token = first_token + jnp.arange(PAIR * rows, dtype=jnp.int32)
+    member = (token[None, :] >= starts[:, None]) & (token[None, :] < ends[:, None])
+    tok_start = jnp.sum(jnp.where(member, starts[:, None], 0), axis=0)
+    position = (token - tok_start).astype(jnp.float32)
+    half = HEAD_WIDTH // 2
+    inverse = ROPE_BASE ** (-(jnp.arange(half, dtype=jnp.float32) * 2.0 / HEAD_WIDTH))
+    angle = position[:, None] * inverse[None, :]
+    cosine, sine = jnp.cos(angle), jnp.sin(angle)
+    cosine = jnp.concatenate([cosine, cosine], axis=1).reshape(PAIR, rows, HEAD_WIDTH)
+    sine = jnp.concatenate([-sine, sine], axis=1).reshape(PAIR, rows, HEAD_WIDTH)
+
+    chosen = choose(prompt_adapter_index, sent["adapters"].reshape(count, 2 * rank, part), chunk)
+    pieces = [
+        jnp.concatenate([in_order(x, kept[:, :chunk], sent["weight x0"]), chosen], axis=0)
+    ]
+
+    def along_z(g, k):
+        return (f"z{g} {k}", pieces[g], functools.partial(shift_z, steps=k))
+
+    def along_y(g, k):
+        return (f"y{g} {k}", sent[f"z{g} {k}"] if k else pieces[g], y_swap)
+
+    def older(value):
+        return lax.ppermute(value, "page", [(p, p + 8) for p in range(count - 8)])
+
+    cuts = (0, rows // 2, rows)
+
+    def normed_part(n):
+        return (f"normed x{n}", normed_own[cuts[n] : cuts[n + 1]], x_swap)
+
+    def normed_on(n):
+        return (f"normed xc{n}", sent[f"normed x{n}"], core_swap)
+
+    sent.run(
+        ["weight x0"],
+        [
+            along_z(0, 1),
+            along_z(0, 3),
+            along_y(0, 0),
+            ("weight x1", mine[:, chunk:], x_swap),
+        ],
+    )
+    sent.run(
+        [],
+        [
+            ("normed c", normed_own, core_swap),
+            (
+                "cache x",
+                jnp.concatenate([cache_part(1 - x, core), cache_core[rows:]], axis=0),
+                x_swap,
+            ),
+        ],
+    )
+    pieces.append(in_order(x, kept[:, chunk:], sent["weight x1"]))
+    sent.run(
+        ["z0 1", "z0 3", "y0 0", "weight x1", "cache x", "normed c"],
+        [
+            along_z(0, 2),
+            along_z(1, 1),
+            along_y(0, 1),
+            along_y(0, 3),
+            along_y(1, 0),
+            normed_part(0),
+        ],
+    )
+    cache_own = jnp.concatenate([cache_part(x, core), cache_core[:rows], sent["cache x"]], axis=0)
+    cosine, sine = sent.tie([cosine, sine], ["y0 1"])
+    sent.run(
+        ["z0 2", "z1 1", "y0 1", "y0 3", "y1 0", "normed x0"],
+        [
+            ("cache z", cache_own, older),
+            along_y(0, 2),
+            along_y(1, 1),
+            normed_part(1),
+            normed_on(0),
+        ],
+    )
+    sent.run(
+        ["cache z", "y0 2", "y1 1", "normed x1", "normed xc0"],
+        [
+            normed_on(1),
+            along_z(1, 3),
+            along_z(1, 2),
+            ("cache y", jnp.where(y == 1, sent["cache z"], cache_own), y_swap),
+        ],
+    )
+    normed = [normed_own, sent["normed c"]]
+    normed += [sent[f"normed {way}{n}"] for way in ("x", "xc") for n in range(2)]
+    layout = ((0, 0), (1, 0)) + tuple((i, cuts[n]) for i in (2, 3) for n in range(2))
+
+    def weights_of(g):
+        return [
+            sent[f"{way}{g} {k}"] if k or way == "y" else pieces[g] for k in order for way in "zy"
+        ]
+
+    members = jnp.arange(PAIR, dtype=jnp.int32)
+    places = [((z - k) % z_count) * 2 + (y ^ dy) for k in order for dy in (0, 1)]
+    numbers = jnp.concatenate(
+        [
+            quarter[None],
+            jnp.stack(places),
+            first_token + (quarter ^ members) * rows,
+            starts,
+            ends,
+        ]
+    ).astype(jnp.int32)
+    weights0 = weights_of(0)
+    partial, up = shrink(numbers, layout, normed, weights0, wq_depth, part, slots, rank)
+    partial = partial + swap(partial, 1)
+    partial = partial + swap(partial, 2)
+    shrunk = partial.astype(jnp.bfloat16)
+
+    def project_part(g, weights, shrunk):
+        return project(
+            numbers, layout, normed, weights, shrunk, up[:, g * chunk : (g + 1) * chunk], cosine, sine
+        )
+
+    def attend_part(g, queries, from_row, tile_rows):
+        count_rows = queries.shape[0] * queries.shape[1]
+        tiles = count_rows // tile_rows
+        here = lax.dynamic_slice_in_dim(tok_start, from_row, count_rows, 0)
+        here = here.reshape(tiles, 1, tile_rows)
+        steps = jnp.concatenate(
+            [
+                first_token + from_row + jnp.arange(tiles, dtype=jnp.int32) * tile_rows,
+                here[:, 0, 0],
+                (quarter ^ members) * rows,
+                (first_token - 2 * PAIR * rows)[None],
+            ]
+        ).astype(jnp.int32)
+        return attend(
+            g * HEAD_WIDTH,
+            steps,
+            here,
+            queries.reshape(tiles, tile_rows, chunk),
+            sent["cache z"],
+            sent["cache y"],
+            cache_own,
+        ).reshape(queries.shape)
+
+    def away(value):
+        return lax.dynamic_slice_in_dim(value, 2 * (1 - x), 2, 0)
+
+    def at_home(value):
+        return lax.dynamic_slice_in_dim(value, 2 * x, 2, 0)
+
+    def home(stay, from_x, g, whole):
+
+        def block(found, which):
+            return lax.dynamic_index_in_dim(found, which, 0, keepdims=False)
+
+        from_core = swap(jnp.stack([block(stay, 1 - core), block(from_x, 1 - core)]), 1)
+        found = (
+            (0, block(stay, core)),
+            (2, block(from_x, core)),
+            (1, from_core[0]),
+            (3, from_core[1]),
+        )
+        for bits, piece in found:
+            low = (quarter ^ bits) * width + g * chunk
+            whole = lax.dynamic_update_slice_in_dim(whole, piece, low, 1)
+        return whole
+
+    queries0 = project_part(0, weights0, shrunk)
+    sent.run(
+        ["cache y", "z1 3", "z1 2"],
+        [along_y(1, 3), along_y(1, 2), ("queries x0", away(queries0), x_swap)],
+    )
+    attended0 = attend_part(0, queries0, 0, PAIR * rows // 3)
+    sent.run([], [("attended x0", away(attended0), x_swap)])
+    (shrunk,) = sent.tie([shrunk], ["queries x0"])
+    queries1 = project_part(1, weights_of(1), shrunk)
+    queries_away = away(queries1)
+    sent.run([], [("queries x1", queries_away, x_swap)])
+    (queries_away,) = sent.tie([queries_away], ["attended x0"])
+    attended_away = attend_part(1, queries_away, 2 * (1 - x) * rows, rows)
+    sent.run([], [("attended x1", attended_away, x_swap)])
+    (queries_home,) = sent.tie([at_home(queries1)], ["queries x1"])
+    attended1 = attend_part(1, queries_home, 2 * x * rows, rows)
+    outs = []
+    for name, parts in (
+        ("queries", (at_home(queries0), queries_home)),
+        ("attended", (at_home(attended0), attended1)),
+    ):
+        whole = jnp.zeros((rows, q_cols), jnp.bfloat16)
+        for g, stay in enumerate(parts):
+            whole = home(stay, sent[f"{name} x{g}"], g, whole)
+        outs.append(whole)
+    return tuple(outs)
+
+
 def solution(mesh):
+    page, head = mesh.shape["page"], mesh.shape["head"]
     return jax.shard_map(
-        body,
+        pair_body if head == 1 and page == 32 else body,
         mesh=mesh,
         in_specs=(
             P("page", None),

time: 715 us -> 352 us (0.49)
  the two profiles are of different devices: /device:TPU:16 before, /device:TPU:9 now
where the time goes in v1:
time: 352 us; the launch traced here: 351 us
  Pallas kernels  120 us (34%)
  waiting for transfers between devices  113 us (32%)
  local copies, waits for them, and re-layouts  52.4 us (15%)
  starting transfers between devices  40.2 us (11%)
  other arithmetic  18.7 us (5%)
  between operations  7.27 us (2%)
    pallas_call x3, Pallas kernels, attend(): pl.pallas_call(functools.partial(attend_kernel, column), grid_spec=pltpu....  84.1 us
    ppermute x6, waiting for transfers between devices, shift_z(): lax.ppermute(value, 'page', [(p, (p + 8 * steps) % count) for p in range(...  49.9 us
    ppermute x29, waiting for transfers between devices, swap(): return lax.ppermute(value, 'page', [(p, p ^ bit) for p in range(count)])  34.2 us
    ppermute x1, waiting for transfers between devices, older(): return lax.ppermute(value, 'page', [(p, p + 8) for p in range(count - 8)])  29.2 us
    pallas_call x2, Pallas kernels, project(): pl.pallas_call(functools.partial(project_kernel, layout, blocks), out_sha...  28.4 us
    ppermute x29, starting transfers between devices, swap(): return lax.ppermute(value, 'page', [(p, p ^ bit) for p in range(count)])  24.5 us
    dynamic_update_slice x16, local copies, waits for them, and re-layouts, home(): whole = lax.dynamic_update_slice_in_dim(whole, piece, low, 1)  18.6 us
  transfers between devices with their start and end apart: 37, of which 12 were waited for; matrix products, arithmetic and copies ran while one was open for 17% of the time, Pallas kernels for 34%

profile of v1, /device:TPU:9, one launch (start us, length us, event | category | flops | bytes accessed | tf_op | source)
XLA Modules:
  0.0 351.4 jit_solution(1837731513712775960)
XLA Ops:
  0.7 1.3 constant_dynamic-slice_fusion.23
  2.8 1.5 collective-permute-done
  4.4 1.2 maximum_select_fusion
  6.5 1.2 collective-permute-start.1
  8.5 5.4 %all-to-all-start = ((bf16[32,32,128]{2,1,0:T(8,128)(2,1)}), bf16[32,32,128]{2,1,0:T(8,128)(2,1)S(1)}, u32[]{:S(2)}, u32[]{:S(2)}) async-start(bf16[32,32,128]{2,1,0:T(8,128)(2,1)} %bitcast.95), calls=%async_computation | async-start | bytes 524288 | tf_op jit(solution)/shard_map/all_to_all | solution.py:564
  20.4 2.6 constant_dynamic-slice_fusion.20
  28.9 2.3 choose.1
  34.4 1.2 collective-permute-start.2
  39.6 2.7 collective-permute-done.2
  43.4 1.9 fusion.14
  46.4 3.8 %collective-permute-done.3.refs_8_ = bf16[576,512]{1,0:T(8,128)(2,1)S(1)} collective-permute-done((bf16[576,512]{1,0:T(8,128)(2,1)S(1)}, bf16[576,512]{1,0:T(8,128)(2,1)S(1)}, u32[]{:S(2)}, u32[]{:S(2)}) %collective-permute-start.3) | collective-permute-done | bytes 589856 | tf_op jit(solution)/shard_map/ppermute | solution.py:160
  50.1 14.3 %collective-permute-done.4.refs_10_ = bf16[576,512]{1,0:T(8,128)(2,1)S(1)} collective-permute-done((bf16[576,512]{1,0:T(8,128)(2,1)S(1)}, bf16[576,512]{1,0:T(8,128)(2,1)S(1)}, u32[]{:S(2)}, u32[]{:S(2)}) %collective-permute-start.4) | collective-permute-done | bytes 589856 | tf_op jit(solution)/shard_map/ppermute | solution.py:160
  68.9 11.6 %collective-permute-done.12.refs_9_ = bf16[576,512]{1,0:T(8,128)(2,1)S(1)} collective-permute-done((bf16[576,512]{1,0:T(8,128)(2,1)}, bf16[576,512]{1,0:T(8,128)(2,1)S(1)}, u32[]{:S(2)}, u32[]{:S(2)}) %collective-permute-start.12) | collective-permute-done | bytes 589856 | tf_op jit(solution)/shard_map/ppermute | solution.py:155
  81.5 2.8 fusion.11
  84.3 1.7 pad_maximum_fusion.2
  86.1 19.1 %collective-permute-done.10.refs_8_ = bf16[512,512]{1,0:T(8,128)(2,1)S(1)} collective-permute-done((bf16[512,512]{1,0:T(8,128)(2,1)}, bf16[512,512]{1,0:T(8,128)(2,1)S(1)}, u32[]{:S(2)}, u32[]{:S(2)}) %collective-permute-start.10) | collective-permute-done | bytes 524320 | tf_op jit(solution)/shard_map/ppermute | solution.py:160
  105.3 1.4 copy-done.3
  106.6 4.2 %collective-permute-start.16 = (bf16[1536,512]{1,0:T(8,128)(2,1)S(1)}, bf16[1536,512]{1,0:T(8,128)(2,1)S(1)}, u32[]{:S(2)}, u32[]{:S(2)}) collective-permute-start(bf16[1536,512]{1,0:T(8,128)(2,1)S(1)} %pad_maximum_fusion.own_ref), channel_id=1, source_target_pairs={{0,8},{1,9},{2,10},{3,11},{4,12},{5,13},{6,14},{7,15},{8,16},{9,17... | collective-permute-start | bytes 4718600 | tf_op jit(solution)/shard_map/ppermute | solution.py:646
  110.8 1.2 collective-permute-start.15
  114.7 29.2 %collective-permute-done.16.older_ref = bf16[1536,512]{1,0:T(8,128)(2,1)S(1)} collective-permute-done((bf16[1536,512]{1,0:T(8,128)(2,1)S(1)}, bf16[1536,512]{1,0:T(8,128)(2,1)S(1)}, u32[]{:S(2)}, u32[]{:S(2)}) %collective-permute-start.16) | collective-permute-done | bytes 1572896 | tf_op jit(solution)/shard_map/ppermute | solution.py:646
  143.8 3.4 broadcast_select_fusion
  147.2 1.6 collective-permute-start.20
  148.8 1.2 collective-permute-start.25
  152.2 4.9 %shrink.1 = (f32[16,1536]{1,0:T(8,128)}, bf16[128,1024]{1,0:T(8,128)(2,1)}) custom-call(s32[29]{0:T(128)} %concatenate.84.numbers, bf16[384,4096]{1,0:T(8,128)(2,1)} %copy-done, bf16[384,4096]{1,0:T(8,128)(2,1)} %collective-permute-done.8.refs_1_, bf16[192,4096]{1,0:T(8,128)(2,1)} %copy-done.3, bf16[192,4096]{1,0:T(8,128)(2,1)} %collective-permute-done.15.refs_3_, ...), custom_call_target="tpu_custom_call" | custom-call | flops 1000 | bytes 1000 | tf_op jit(solution)/shard_map/shrink/pallas_call | solution.py:296
  157.5 3.3 collective-permute-start.24
  161.7 1.2 collective-permute-start.22
  163.0 1.7 fusion.19
  166.3 14.2 %project.2 = bf16[4,384,512]{2,1,0:T(8,128)(2,1)} custom-call(s32[29]{0:T(128)} %concatenate.84.numbers, bf16[384,4096]{1,0:T(8,128)(2,1)} %copy-done, bf16[384,4096]{1,0:T(8,128)(2,1)} %collective-permute-done.8.refs_1_, bf16[192,4096]{1,0:T(8,128)(2,1)} %copy-done.3, bf16[192,4096]{1,0:T(8,128)(2,1)} %collective-permute-done.15.refs_3_, ...), custom_call_target="tpu_custom_call" | custom-call | flops 1000 | bytes 1000 | tf_op jit(solution)/shard_map/project/pallas_call | solution.py:371
  181.7 12.7 %collective-permute-done.24.refs_12_ = bf16[512,512]{1,0:T(8,128)(2,1)} collective-permute-done((bf16[512,512]{1,0:T(8,128)(2,1)S(1)}, bf16[512,512]{1,0:T(8,128)(2,1)}, u32[]{:S(2)}, u32[]{:S(2)}) %collective-permute-start.24) | collective-permute-done | bytes 524320 | tf_op jit(solution)/shard_map/ppermute | solution.py:160
  196.2 38.0 %attend.3 = bf16[3,512,512]{2,1,0:T(8,128)(2,1)} custom-call(s32[11]{0:T(128)} %pad_add_fusion.numbers, s32[3,1,512]{2,1,0:T(1,128)} %copy-done.30, bf16[3,512,512]{2,1,0:T(8,128)(2,1)} %bitcast.84, bf16[1536,512]{1,0:T(8,128)(2,1)} %copy-done.1, bf16[1536,512]{1,0:T(8,128)(2,1)} %collective-permute-done.25.old_ref, bf16[1536,512]{1,0:T(8,128)(2,1)} %copy-done.2), custom_call_target="tpu_custom_call" | custom-call | flops 1000 | bytes 1000 | tf_op jit(solution)/shard_map/attend/pallas_call | solution.py:490
  234.3 1.2 constant_dynamic-slice_fusion.4
  235.8 1.5 collective-permute-start.29
  239.0 2.0 broadcast.81.clone.1
  241.1 1.8 bitcast_dynamic-update-slice_fusion.3
  242.9 5.7 %collective-permute-done.28.refs_11_ = bf16[512,512]{1,0:T(8,128)(2,1)} collective-permute-done((bf16[512,512]{1,0:T(8,128)(2,1)}, bf16[512,512]{1,0:T(8,128)(2,1)}, u32[]{:S(2)}, u32[]{:S(2)}) %collective-permute-start.28) | collective-permute-done | bytes 524320 | tf_op jit(solution)/shard_map/ppermute | solution.py:155
  248.5 11.2 %collective-permute-done.29.refs_13_ = bf16[512,512]{1,0:T(8,128)(2,1)} collective-permute-done((bf16[512,512]{1,0:T(8,128)(2,1)}, bf16[512,512]{1,0:T(8,128)(2,1)}, u32[]{:S(2)}, u32[]{:S(2)}) %collective-permute-start.29) | collective-permute-done | bytes 524320 | tf_op jit(solution)/shard_map/ppermute | solution.py:155
  259.7 14.2 %project.3 = bf16[4,384,512]{2,1,0:T(8,128)(2,1)} custom-call(s32[29]{0:T(128)} %concatenate.84.numbers, bf16[384,4096]{1,0:T(8,128)(2,1)} %copy-done, bf16[384,4096]{1,0:T(8,128)(2,1)} %collective-permute-done.8.refs_1_, bf16[192,4096]{1,0:T(8,128)(2,1)} %copy-done.3, bf16[192,4096]{1,0:T(8,128)(2,1)} %collective-permute-done.15.refs_3_, ...), custom_call_target="tpu_custom_call" | custom-call | flops 1000 | bytes 1000 | tf_op jit(solution)/shard_map/project/pallas_call | solution.py:371
  274.0 2.4 constant_dynamic-slice_fusion.7
  278.0 1.7 copy-done.13
  279.7 25.0 %attend.5 = bf16[2,384,512]{2,1,0:T(8,128)(2,1)} custom-call(s32[9]{0:T(128)} %get-tuple-element.146.numbers, s32[2,1,384]{2,1,0:T(1,128)} %copy-done.32, bf16[2,384,512]{2,1,0:T(8,128)(2,1)} %copy-done.11, bf16[1536,512]{1,0:T(8,128)(2,1)} %copy-done.1, bf16[1536,512]{1,0:T(8,128)(2,1)} %collective-permute-done.25.old_ref, bf16[1536,512]{1,0:T(8,128)(2,1)} %copy-done.2), custom_call_target="tpu_custom_call" | custom-call | flops 1000 | bytes 1000 | tf_op jit(solution)/shard_map/attend/pallas_call | solution.py:490
  305.9 2.3 collective-permute-start.33
  309.4 1.8 bitcast_dynamic-update-slice_fusion.2
  311.1 1.8 bitcast_dynamic-update-slice_fusion.6
  312.9 21.0 %attend.4 = bf16[2,384,512]{2,1,0:T(8,128)(2,1)} custom-call(s32[9]{0:T(128)} %get-tuple-element.147.numbers, s32[2,1,384]{2,1,0:T(1,128)} %copy-done.31, bf16[2,384,512]{2,1,0:T(8,128)(2,1)} %get-tuple-element.106.query_ref, bf16[1536,512]{1,0:T(8,128)(2,1)} %copy-done.1, bf16[1536,512]{1,0:T(8,128)(2,1)} %collective-permute-done.25.old_ref, ...), custom_call_target="tpu_custom_call" | custom-call | flops 1000 | bytes 1000 | tf_op jit(solution)/shard_map/attend/pallas_call | solution.py:490
  338.1 1.8 fusion.6
  339.9 1.8 fusion.5
  344.7 1.8 bitcast_dynamic-update-slice_fusion.4
  346.5 1.8 bitcast_dynamic-update-slice_fusion
  (196 shorter events, 50.8 us)
Async XLA Ops:
  2.1 2.3 collective-permute-start
  2.8 15.6 %copy-start.33 = (bf16[4096]{0:T(1024)(128)(2,1)S(1)}, bf16[4096]{0:T(1024)(128)(2,1)}, u32[]{:S(2)}) copy-start(bf16[4096]{0:T(1024)(128)(2,1)} %param.10) | copy-start | bytes 24580
  6.5 13.9 %collective-permute-start.1 = (bf16[256,512]{1,0:T(8,128)(2,1)}, bf16[256,512]{1,0:T(8,128)(2,1)}, u32[]{:S(2)}, u32[]{:S(2)}) collective-permute-start(bf16[256,512]{1,0:T(8,128)(2,1)} %get-tuple-element.136), channel_id=1, source_target_pairs={{0,2},{1,3},{2,0},{3,1},{4,6},{5,7},{6,4},{7,5},{8,10},{9,11},{10,... | collective-permute-start | bytes 786440 | tf_op jit(solution)/shard_map/ppermute | solution.py:155
  7.7 15.5 %copy-start.5 = (bf16[384,4096]{1,0:T(8,128)(2,1)S(1)}, bf16[384,4096]{1,0:T(8,128)(2,1)}, u32[]{:S(2)}) copy-start(bf16[384,4096]{1,0:T(8,128)(2,1)} %param.9) | copy-start | bytes 9437188
  8.5 19.7 %all-to-all-start = ((bf16[32,32,128]{2,1,0:T(8,128)(2,1)}), bf16[32,32,128]{2,1,0:T(8,128)(2,1)S(1)}, u32[]{:S(2)}, u32[]{:S(2)}) async-start(bf16[32,32,128]{2,1,0:T(8,128)(2,1)} %bitcast.95), calls=%async_computation | async-start | bytes 524288 | tf_op jit(solution)/shard_map/all_to_all | solution.py:564
  25.0 18.4 %copy-start = (bf16[384,4096]{1,0:T(8,128)(2,1)}, bf16[384,4096]{1,0:T(8,128)(2,1)S(1)}, u32[]{:S(2)}) copy-start(bf16[384,4096]{1,0:T(8,128)(2,1)S(1)} %fusion.2.refs_0_) | copy-start | bytes 9437188
  25.0 39.5 %collective-permute-start.8 = (bf16[384,4096]{1,0:T(8,128)(2,1)S(1)}, bf16[384,4096]{1,0:T(8,128)(2,1)}, u32[]{:S(2)}, u32[]{:S(2)}) collective-permute-start(bf16[384,4096]{1,0:T(8,128)(2,1)S(1)} %fusion.2.refs_0_), channel_id=1, source_target_pairs={{0,1},{1,0},{2,3},{3,2},{4,5},{5,4},{6,7},{7,6},{8,9},{9,8},{10,11... | collective-permute-start | bytes 9437192 | tf_op jit(solution)/shard_map/ppermute | solution.py:155
  27.9 9.3 %collective-permute-start.6 = (bf16[768,512]{1,0:T(8,128)(2,1)}, bf16[768,512]{1,0:T(8,128)(2,1)}, u32[]{:S(2)}, u32[]{:S(2)}) collective-permute-start(bf16[768,512]{1,0:T(8,128)(2,1)} %maximum_maximum_fusion), channel_id=1, source_target_pairs={{0,1},{1,0},{2,3},{3,2},{4,5},{5,4},{6,7},{7,6},{8,9},{9,8},{10,11... | collective-permute-start | bytes 2359304 | tf_op jit(solution)/shard_map/ppermute | solution.py:155
  34.4 7.8 %collective-permute-start.2 = (bf16[256,512]{1,0:T(8,128)(2,1)S(1)}, bf16[256,512]{1,0:T(8,128)(2,1)S(1)}, u32[]{:S(2)}, u32[]{:S(2)}) collective-permute-start(bf16[256,512]{1,0:T(8,128)(2,1)S(1)} %copy-done.27), channel_id=1, source_target_pairs={{0,2},{1,3},{2,0},{3,1},{4,6},{5,7},{6,4},{7,5},{8,10},{9,11},{10,... | collective-permute-start | bytes 786440 | tf_op jit(solution)/shard_map/ppermute | solution.py:155
  35.7 14.5 %collective-permute-start.3 = (bf16[576,512]{1,0:T(8,128)(2,1)S(1)}, bf16[576,512]{1,0:T(8,128)(2,1)S(1)}, u32[]{:S(2)}, u32[]{:S(2)}) collective-permute-start(bf16[576,512]{1,0:T(8,128)(2,1)S(1)} %pad_maximum_fusion.8.refs_6_), channel_id=1, source_target_pairs={{0,8},{1,9},{2,10},{3,11},{4,12},{5,13},{6,14},{7,15},{8,16},{9,17... | collective-permute-start | bytes 1769480 | tf_op jit(solution)/shard_map/ppermute | solution.py:160
  36.9 27.6 %collective-permute-start.4 = (bf16[576,512]{1,0:T(8,128)(2,1)S(1)}, bf16[576,512]{1,0:T(8,128)(2,1)S(1)}, u32[]{:S(2)}, u32[]{:S(2)}) collective-permute-start(bf16[576,512]{1,0:T(8,128)(2,1)S(1)} %pad_maximum_fusion.8.refs_6_), channel_id=1, source_target_pairs={{0,24},{1,25},{2,26},{3,27},{4,28},{5,29},{6,30},{7,31},{8,0},{9,1... | collective-permute-start | bytes 1769480 | tf_op jit(solution)/shard_map/ppermute | solution.py:160
  37.2 27.3 %collective-permute-start.5 = (bf16[576,512]{1,0:T(8,128)(2,1)S(1)}, bf16[576,512]{1,0:T(8,128)(2,1)S(1)}, u32[]{:S(2)}, u32[]{:S(2)}) collective-permute-start(bf16[576,512]{1,0:T(8,128)(2,1)S(1)} %pad_maximum_fusion.8.refs_6_), channel_id=1, source_target_pairs={{0,4},{1,5},{2,6},{3,7},{4,0},{5,1},{6,2},{7,3},{8,12},{9,13},{10,... | collective-permute-start | bytes 1769480 | tf_op jit(solution)/shard_map/ppermute | solution.py:155
  39.6 26.1 %copy-start.36 = (s32[8]{0:T(128)S(1)}, s32[8]{0:T(128)}, u32[]{:S(2)}) copy-start(s32[8]{0:T(128)} %param.16) | copy-start | bytes 100
  42.3 22.2 %collective-permute-start.7 = (bf16[768,512]{1,0:T(8,128)(2,1)S(1)}, bf16[768,512]{1,0:T(8,128)(2,1)S(1)}, u32[]{:S(2)}, u32[]{:S(2)}) collective-permute-start(bf16[768,512]{1,0:T(8,128)(2,1)S(1)} %pad_maximum_fusion.1), channel_id=1, source_target_pairs={{0,2},{1,3},{2,0},{3,1},{4,6},{5,7},{6,4},{7,5},{8,10},{9,11},{10,... | collective-permute-start | bytes 2359304 | tf_op jit(solution)/shard_map/ppermute | solution.py:155
  50.1 15.3 %copy-start.14 = (bf16[576,512]{1,0:T(8,128)(2,1)}, bf16[576,512]{1,0:T(8,128)(2,1)S(1)}, u32[]{:S(2)}) copy-start(bf16[576,512]{1,0:T(8,128)(2,1)S(1)} %collective-permute-done.3.refs_8_) | copy-start | bytes 1769476
  65.4 39.8 %collective-permute-start.11 = (bf16[192,4096]{1,0:T(8,128)(2,1)}, bf16[192,4096]{1,0:T(8,128)(2,1)S(1)}, u32[]{:S(2)}, u32[]{:S(2)}) collective-permute-start(bf16[192,4096]{1,0:T(8,128)(2,1)} %get-tuple-element.68), channel_id=1, source_target_pairs={{0,2},{1,3},{2,0},{3,1},{4,6},{5,7},{6,4},{7,5},{8,10},{9,11},{10,... | collective-permute-start | bytes 4718600 | tf_op jit(solution)/shard_map/ppermute | solution.py:155
  65.9 14.6 %collective-permute-start.12 = (bf16[576,512]{1,0:T(8,128)(2,1)}, bf16[576,512]{1,0:T(8,128)(2,1)S(1)}, u32[]{:S(2)}, u32[]{:S(2)}) collective-permute-start(bf16[576,512]{1,0:T(8,128)(2,1)} %copy-done.14), channel_id=1, source_target_pairs={{0,4},{1,5},{2,6},{3,7},{4,0},{5,1},{6,2},{7,3},{8,12},{9,13},{10,... | collective-permute-start | bytes 1769480 | tf_op jit(solution)/shard_map/ppermute | solution.py:155
  67.2 18.7 %copy-start.10 = (bf16[768,512]{1,0:T(8,128)(2,1)S(1)}, bf16[768,512]{1,0:T(8,128)(2,1)}, u32[]{:S(2)}) copy-start(bf16[768,512]{1,0:T(8,128)(2,1)} %copy-done.9) | copy-start | bytes 2359300
  67.2 18.7 %copy-start.20 = (bf16[384,256]{1,0:T(8,128)(2,1)S(1)}, bf16[384,256]{1,0:T(8,128)(2,1)}, u32[]{:S(2)}) copy-start(bf16[384,256]{1,0:T(8,128)(2,1)} %get-tuple-element.116) | copy-start | bytes 589828
  67.2 18.7 %copy-start.21 = (bf16[384,256]{1,0:T(8,128)(2,1)S(1)}, bf16[384,256]{1,0:T(8,128)(2,1)}, u32[]{:S(2)}) copy-start(bf16[384,256]{1,0:T(8,128)(2,1)} %get-tuple-element.117) | copy-start | bytes 589828
  67.3 38.0 %collective-permute-start.13 = (bf16[576,512]{1,0:T(8,128)(2,1)}, bf16[576,512]{1,0:T(8,128)(2,1)S(1)}, u32[]{:S(2)}, u32[]{:S(2)}) collective-permute-start(bf16[576,512]{1,0:T(8,128)(2,1)} %copy-done.15), channel_id=1, source_target_pairs={{0,4},{1,5},{2,6},{3,7},{4,0},{5,1},{6,2},{7,3},{8,12},{9,13},{10,... | collective-permute-start | bytes 1769480 | tf_op jit(solution)/shard_map/ppermute | solution.py:155
  67.6 37.6 %collective-permute-start.9 = (bf16[576,512]{1,0:T(8,128)(2,1)}, bf16[576,512]{1,0:T(8,128)(2,1)}, u32[]{:S(2)}, u32[]{:S(2)}) collective-permute-start(bf16[576,512]{1,0:T(8,128)(2,1)} %copy-done.8), channel_id=1, source_target_pairs={{0,16},{1,17},{2,18},{3,19},{4,20},{5,21},{6,22},{7,23},{8,24},{9,... | collective-permute-start | bytes 1769480 | tf_op jit(solution)/shard_map/ppermute | solution.py:160
  68.0 37.2 %collective-permute-start.10 = (bf16[512,512]{1,0:T(8,128)(2,1)}, bf16[512,512]{1,0:T(8,128)(2,1)S(1)}, u32[]{:S(2)}, u32[]{:S(2)}) collective-permute-start(bf16[512,512]{1,0:T(8,128)(2,1)} %maximum_select_fusion.3.refs_6_), channel_id=1, source_target_pairs={{0,8},{1,9},{2,10},{3,11},{4,12},{5,13},{6,14},{7,15},{8,16},{9,17... | collective-permute-start | bytes 1572872 | tf_op jit(solution)/shard_map/ppermute | solution.py:160
  80.5 24.7 %collective-permute-start.14 = (bf16[512,512]{1,0:T(8,128)(2,1)}, bf16[512,512]{1,0:T(8,128)(2,1)S(1)}, u32[]{:S(2)}, u32[]{:S(2)}) collective-permute-start(bf16[512,512]{1,0:T(8,128)(2,1)} %maximum_select_fusion.3.refs_6_), channel_id=1, source_target_pairs={{0,4},{1,5},{2,6},{3,7},{4,0},{5,1},{6,2},{7,3},{8,12},{9,13},{10,... | collective-permute-start | bytes 1572872 | tf_op jit(solution)/shard_map/ppermute | solution.py:155
  86.1 70.9 %copy-start.2 = (bf16[1536,512]{1,0:T(8,128)(2,1)}, bf16[1536,512]{1,0:T(8,128)(2,1)S(1)}, u32[]{:S(2)}) copy-start(bf16[1536,512]{1,0:T(8,128)(2,1)S(1)} %pad_maximum_fusion.own_ref) | copy-start | bytes 4718596
  106.6 37.2 %collective-permute-start.16 = (bf16[1536,512]{1,0:T(8,128)(2,1)S(1)}, bf16[1536,512]{1,0:T(8,128)(2,1)S(1)}, u32[]{:S(2)}, u32[]{:S(2)}) collective-permute-start(bf16[1536,512]{1,0:T(8,128)(2,1)S(1)} %pad_maximum_fusion.own_ref), channel_id=1, source_target_pairs={{0,8},{1,9},{2,10},{3,11},{4,12},{5,13},{6,14},{7,15},{8,16},{9,17... | collective-permute-start | bytes 4718600 | tf_op jit(solution)/shard_map/ppermute | solution.py:646
  110.8 36.4 %collective-permute-start.15 = (bf16[192,4096]{1,0:T(8,128)(2,1)}, bf16[192,4096]{1,0:T(8,128)(2,1)}, u32[]{:S(2)}, u32[]{:S(2)}) collective-permute-start(bf16[192,4096]{1,0:T(8,128)(2,1)} %get-tuple-element.74), channel_id=1, source_target_pairs={{0,2},{1,3},{2,0},{3,1},{4,6},{5,7},{6,4},{7,5},{8,10},{9,11},{10,... | collective-permute-start | bytes 4718600 | tf_op jit(solution)/shard_map/ppermute | solution.py:155
  112.1 35.1 %collective-permute-start.19 = (bf16[192,4096]{1,0:T(8,128)(2,1)}, bf16[192,4096]{1,0:T(8,128)(2,1)}, u32[]{:S(2)}, u32[]{:S(2)}) collective-permute-start(bf16[192,4096]{1,0:T(8,128)(2,1)} %copy-done.3), channel_id=1, source_target_pairs={{0,1},{1,0},{2,3},{3,2},{4,5},{5,4},{6,7},{7,6},{8,9},{9,8},{10,11... | collective-permute-start | bytes 4718600 | tf_op jit(solution)/shard_map/ppermute | solution.py:155
  113.2 34.0 %collective-permute-start.17 = (bf16[576,512]{1,0:T(8,128)(2,1)}, bf16[576,512]{1,0:T(8,128)(2,1)}, u32[]{:S(2)}, u32[]{:S(2)}) collective-permute-start(bf16[576,512]{1,0:T(8,128)(2,1)} %collective-permute-done.9.refs_12_), channel_id=1, source_target_pairs={{0,4},{1,5},{2,6},{3,7},{4,0},{5,1},{6,2},{7,3},{8,12},{9,13},{10,... | collective-permute-start | bytes 1769480 | tf_op jit(solution)/shard_map/ppermute | solution.py:155
  114.4 32.8 %collective-permute-start.18 = (bf16[512,512]{1,0:T(8,128)(2,1)}, bf16[512,512]{1,0:T(8,128)(2,1)}, u32[]{:S(2)}, u32[]{:S(2)}) collective-permute-start(bf16[512,512]{1,0:T(8,128)(2,1)} %copy-done.25), channel_id=1, source_target_pairs={{0,4},{1,5},{2,6},{3,7},{4,0},{5,1},{6,2},{7,3},{8,12},{9,13},{10,... | collective-permute-start | bytes 1572872 | tf_op jit(solution)/shard_map/ppermute | solution.py:155
  147.2 4.9 %collective-permute-start.20 = (bf16[192,4096]{1,0:T(8,128)(2,1)}, bf16[192,4096]{1,0:T(8,128)(2,1)}, u32[]{:S(2)}, u32[]{:S(2)}) collective-permute-start(bf16[192,4096]{1,0:T(8,128)(2,1)} %collective-permute-done.15.refs_3_), channel_id=1, source_target_pairs={{0,1},{1,0},{2,3},{3,2},{4,5},{5,4},{6,7},{7,6},{8,9},{9,8},{10,11... | collective-permute-start | bytes 4718600 | tf_op jit(solution)/shard_map/ppermute | solution.py:155
  148.8 45.6 %collective-permute-start.25 = (bf16[1536,512]{1,0:T(8,128)(2,1)}, bf16[1536,512]{1,0:T(8,128)(2,1)}, u32[]{:S(2)}, u32[]{:S(2)}) collective-permute-start(bf16[1536,512]{1,0:T(8,128)(2,1)} %broadcast_select_fusion), channel_id=1, source_target_pairs={{0,4},{1,5},{2,6},{3,7},{4,0},{5,1},{6,2},{7,3},{8,12},{9,13},{10,... | collective-permute-start | bytes 4718600 | tf_op jit(solution)/shard_map/ppermute | solution.py:155
  157.1 3.7 %collective-permute-start.21 = (f32[16,1536]{1,0:T(8,128)}, f32[16,1536]{1,0:T(8,128)S(1)}, u32[]{:S(2)}, u32[]{:S(2)}) collective-permute-start(f32[16,1536]{1,0:T(8,128)} %get-tuple-element.89), channel_id=1, source_target_pairs={{0,1},{1,0},{2,3},{3,2},{4,5},{5,4},{6,7},{7,6},{8,9},{9,8},{10,11... | collective-permute-start | bytes 294920 | tf_op jit(solution)/shard_map/ppermute | solution.py:155
  157.5 24.2 %collective-permute-start.23 = (bf16[512,512]{1,0:T(8,128)(2,1)S(1)}, bf16[512,512]{1,0:T(8,128)(2,1)}, u32[]{:S(2)}, u32[]{:S(2)}) collective-permute-start(bf16[512,512]{1,0:T(8,128)(2,1)S(1)} %copy-done.19), channel_id=1, source_target_pairs={{0,24},{1,25},{2,26},{3,27},{4,28},{5,29},{6,30},{7,31},{8,0},{9,1... | collective-permute-start | bytes 1572872 | tf_op jit(solution)/shard_map/ppermute | solution.py:160
  157.5 36.8 %collective-permute-start.24 = (bf16[512,512]{1,0:T(8,128)(2,1)S(1)}, bf16[512,512]{1,0:T(8,128)(2,1)}, u32[]{:S(2)}, u32[]{:S(2)}) collective-permute-start(bf16[512,512]{1,0:T(8,128)(2,1)S(1)} %copy-done.19), channel_id=1, source_target_pairs={{0,16},{1,17},{2,18},{3,19},{4,20},{5,21},{6,22},{7,23},{8,24},{9,... | collective-permute-start | bytes 1572872 | tf_op jit(solution)/shard_map/ppermute | solution.py:160
  161.7 3.9 %collective-permute-start.22 = (f32[16,1536]{1,0:T(8,128)S(1)}, f32[16,1536]{1,0:T(8,128)S(1)}, u32[]{:S(2)}, u32[]{:S(2)}) collective-permute-start(f32[16,1536]{1,0:T(8,128)S(1)} %add.361), channel_id=1, source_target_pairs={{0,2},{1,3},{2,0},{3,1},{4,6},{5,7},{6,4},{7,5},{8,10},{9,11},{10,... | collective-permute-start | bytes 294920 | tf_op jit(solution)/shard_map/ppermute | solution.py:155
  194.4 48.5 %collective-permute-start.26 = (bf16[2,384,512]{2,1,0:T(8,128)(2,1)S(1)}, bf16[2,384,512]{2,1,0:T(8,128)(2,1)}, u32[]{:S(2)}, u32[]{:S(2)}) collective-permute-start(bf16[2,384,512]{2,1,0:T(8,128)(2,1)S(1)} %constant_dynamic-slice_fusion.11), channel_id=1, source_target_pairs={{0,2},{1,3},{2,0},{3,1},{4,6},{5,7},{6,4},{7,5},{8,10},{9,11},{10,... | collective-permute-start | bytes 2359304 | tf_op jit(solution)/shard_map/ppermute | solution.py:155
  196.2 41.1 %copy-start.35 = (s32[2]{0:T(128)S(1)}, s32[2]{0:T(128)}, u32[]{:S(2)}) copy-start(s32[2]{0:T(128)} %get-tuple-element.152) | copy-start | bytes 28
  196.2 42.8 %copy-start.4 = (bf16[4,384,512]{2,1,0:T(8,128)(2,1)S(1)}, bf16[4,384,512]{2,1,0:T(8,128)(2,1)}, u32[]{:S(2)}) copy-start(bf16[4,384,512]{2,1,0:T(8,128)(2,1)} %project.2) | copy-start | bytes 4718596
  235.5 44.2 %collective-permute-start.32 = (bf16[2,384,512]{2,1,0:T(8,128)(2,1)S(1)}, bf16[2,384,512]{2,1,0:T(8,128)(2,1)}, u32[]{:S(2)}, u32[]{:S(2)}) collective-permute-start(bf16[2,384,512]{2,1,0:T(8,128)(2,1)S(1)} %constant_dynamic-slice_fusion.4), channel_id=1, source_target_pairs={{0,2},{1,3},{2,0},{3,1},{4,6},{5,7},{6,4},{7,5},{8,10},{9,11},{10,... | collective-permute-start | bytes 2359304 | tf_op jit(solution)/shard_map/ppermute | solution.py:155
  235.8 12.7 %collective-permute-start.28 = (bf16[512,512]{1,0:T(8,128)(2,1)}, bf16[512,512]{1,0:T(8,128)(2,1)}, u32[]{:S(2)}, u32[]{:S(2)}) collective-permute-start(bf16[512,512]{1,0:T(8,128)(2,1)} %collective-permute-done.23.refs_10_), channel_id=1, source_target_pairs={{0,4},{1,5},{2,6},{3,7},{4,0},{5,1},{6,2},{7,3},{8,12},{9,13},{10,... | collective-permute-start | bytes 1572872 | tf_op jit(solution)/shard_map/ppermute | solution.py:155
  235.8 23.9 %collective-permute-start.29 = (bf16[512,512]{1,0:T(8,128)(2,1)}, bf16[512,512]{1,0:T(8,128)(2,1)}, u32[]{:S(2)}, u32[]{:S(2)}) collective-permute-start(bf16[512,512]{1,0:T(8,128)(2,1)} %collective-permute-done.24.refs_12_), channel_id=1, source_target_pairs={{0,4},{1,5},{2,6},{3,7},{4,0},{5,1},{6,2},{7,3},{8,12},{9,13},{10,... | collective-permute-start | bytes 1572872 | tf_op jit(solution)/shard_map/ppermute | solution.py:155
  276.4 36.5 %collective-permute-start.30 = (bf16[2,384,512]{2,1,0:T(8,128)(2,1)S(1)}, bf16[2,384,512]{2,1,0:T(8,128)(2,1)}, u32[]{:S(2)}, u32[]{:S(2)}) collective-permute-start(bf16[2,384,512]{2,1,0:T(8,128)(2,1)S(1)} %get-tuple-element.111.query_ref), channel_id=1, source_target_pairs={{0,2},{1,3},{2,0},{3,1},{4,6},{5,7},{6,4},{7,5},{8,10},{9,11},{10,... | collective-permute-start | bytes 2359304 | tf_op jit(solution)/shard_map/ppermute | solution.py:155
  304.7 30.4 %collective-permute-start.34 = (bf16[2,384,512]{2,1,0:T(8,128)(2,1)}, bf16[2,384,512]{2,1,0:T(8,128)(2,1)}, u32[]{:S(2)}, u32[]{:S(2)}) collective-permute-start(bf16[2,384,512]{2,1,0:T(8,128)(2,1)} %attend.5), channel_id=1, source_target_pairs={{0,2},{1,3},{2,0},{3,1},{4,6},{5,7},{6,4},{7,5},{8,10},{9,11},{10,... | collective-permute-start | bytes 2359304 | tf_op jit(solution)/shard_map/ppermute | solution.py:155
  305.9 32.2 %collective-permute-start.33 = (bf16[2,384,512]{2,1,0:T(8,128)(2,1)S(1)}, bf16[2,384,512]{2,1,0:T(8,128)(2,1)}, u32[]{:S(2)}, u32[]{:S(2)}) collective-permute-start(bf16[2,384,512]{2,1,0:T(8,128)(2,1)S(1)} %pad_maximum_fusion.6), channel_id=1, source_target_pairs={{0,1},{1,0},{2,3},{3,2},{4,5},{5,4},{6,7},{7,6},{8,9},{9,8},{10,11... | collective-permute-start | bytes 2359304 | tf_op jit(solution)/shard_map/ppermute | solution.py:155
  309.3 32.4 %collective-permute-start.27 = (bf16[2,384,512]{2,1,0:T(8,128)(2,1)S(1)}, bf16[2,384,512]{2,1,0:T(8,128)(2,1)S(1)}, u32[]{:S(2)}, u32[]{:S(2)}) collective-permute-start(bf16[2,384,512]{2,1,0:T(8,128)(2,1)S(1)} %pad_maximum_fusion.4), channel_id=1, source_target_pairs={{0,1},{1,0},{2,3},{3,2},{4,5},{5,4},{6,7},{7,6},{8,9},{9,8},{10,11... | collective-permute-start | bytes 2359304 | tf_op jit(solution)/shard_map/ppermute | solution.py:155
  336.3 12.0 %collective-permute-start.35 = (bf16[2,384,512]{2,1,0:T(8,128)(2,1)S(1)}, bf16[2,384,512]{2,1,0:T(8,128)(2,1)S(1)}, u32[]{:S(2)}, u32[]{:S(2)}) collective-permute-start(bf16[2,384,512]{2,1,0:T(8,128)(2,1)S(1)} %pad_maximum_fusion.7), channel_id=1, source_target_pairs={{0,1},{1,0},{2,3},{3,2},{4,5},{5,4},{6,7},{7,6},{8,9},{9,8},{10,11... | collective-permute-start | bytes 2359304 | tf_op jit(solution)/shard_map/ppermute | solution.py:155
  337.9 11.9 %collective-permute-start.31 = (bf16[2,384,512]{2,1,0:T(8,128)(2,1)S(1)}, bf16[2,384,512]{2,1,0:T(8,128)(2,1)S(1)}, u32[]{:S(2)}, u32[]{:S(2)}) collective-permute-start(bf16[2,384,512]{2,1,0:T(8,128)(2,1)S(1)} %pad_maximum_fusion.5), channel_id=1, source_target_pairs={{0,1},{1,0},{2,3},{3,2},{4,5},{5,4},{6,7},{7,6},{8,9},{9,8},{10,11... | collective-permute-start | bytes 2359304 | tf_op jit(solution)/shard_map/ppermute | solution.py:155
  (26 other events, 134.8 us)

commit v2 on v1

--- a/solution.py
+++ b/solution.py
@@ -16,6 +16,7 @@
 ROPE_BASE = 500000.0
 KEY_TILE = 512
 LOWEST = -1e30
+SAFE_POWER = 90.0
 
 
 def from_behind(value, axis, steps):
@@ -237,15 +238,14 @@
     )(which, every)
 
 
-def shrink_kernel(layout, blocks, depth, part, numbers, *refs):
+def shrink_kernel(layout, blocks, part, numbers, *refs):
     normed_refs, refs = refs[: len(layout)], refs[len(layout) :]
-    weight_refs, refs = refs[:blocks], refs[blocks:]
-    out_ref, up_ref, held, adapters, normed_sems, sems = refs
+    near_ref, far_ref, out_ref, up_ref, held, adapters, normed_sems, sems = refs
     rank, columns = out_ref.shape
     rows = columns // PAIR
     features = held.shape[2]
     slots = adapters.shape[0] // (2 * rank)
-    extra = weight_refs[0].shape[0] - depth
+    extra = near_ref.shape[0] * 2 // blocks
     quarter = numbers[0]
     columns_here = pl.ds(pl.multiple_of(quarter * features, features), features)
     copies = [
@@ -256,10 +256,11 @@
     ]
     for b in range(blocks):
         place = pl.multiple_of(numbers[1 + b] * part, part)
+        source = (near_ref, far_ref)[b % 2].at[pl.ds(b // 2 * extra, extra)]
         for h in range(2 * slots * rank // extra):
             copies.append(
                 pltpu.make_async_copy(
-                    weight_refs[b].at[pl.ds(depth, extra), pl.ds(h * part, part)],
+                    source.at[:, pl.ds(h * part, part)],
                     adapters.at[pl.ds(h * extra, extra), pl.ds(place, part)],
                     sems.at[b, h],
                 )
@@ -288,19 +289,18 @@
         out_ref[:, pl.ds(place, rows)] = found
 
 
-def shrink(numbers, layout, normed, weights, depth, part, slots, rank):
+def shrink(numbers, layout, normed, near, far, blocks, part, slots, rank):
     rows, _ = normed[0].shape
-    blocks = len(weights)
-    extra, width = weights[0].shape[0] - depth, blocks * part
+    extra, width = near.shape[0] * 2 // blocks, blocks * part
     vmem = pl.BlockSpec(memory_space=pltpu.VMEM)
     return pl.pallas_call(
-        functools.partial(shrink_kernel, layout, blocks, depth, part),
+        functools.partial(shrink_kernel, layout, blocks, part),
         out_shape=(
             jax.ShapeDtypeStruct((rank, PAIR * rows), jnp.float32),
             jax.ShapeDtypeStruct((slots * rank, width), jnp.bfloat16),
         ),
         in_specs=[pl.BlockSpec(memory_space=pltpu.SMEM)]
-        + [pl.BlockSpec(memory_space=pl.ANY)] * (len(layout) + blocks),
+        + [pl.BlockSpec(memory_space=pl.ANY)] * (len(layout) + 2),
         out_specs=(vmem, vmem),
         scratch_shapes=[
             pltpu.VMEM((PAIR, rows, width), jnp.bfloat16),
@@ -311,21 +311,22 @@
         compiler_params=pltpu.CompilerParams(vmem_limit_bytes=60 * 1024 * 1024),
         cost_estimate=pl.CostEstimate(flops=1000, bytes_accessed=1000, transcendentals=0),
         name="shrink",
-    )(numbers, *normed, *weights)
-
-
-def project_kernel(layout, blocks, numbers, *refs):
+    )(numbers, *normed, near, far)
+
+
+def project_kernel(layout, spots, numbers, *refs):
+    blocks = len(spots)
+    arrays = 1 + max(which for which, _ in spots)
     normed_refs, refs = refs[: len(layout)], refs[len(layout) :]
-    weight_refs, refs = refs[:blocks], refs[blocks:]
-    shrunk_ref, up_ref, cosine_ref, sine_ref, out_ref, held, weight, sems = refs
-    width = out_ref.shape[2]
-    rows = out_ref.shape[1]
+    weight_refs, refs = refs[:arrays], refs[arrays:]
+    shrunk_ref, up_ref, cosine_ref, sine_ref, home_ref, away_ref, held, weight, sems = refs
+    _, rows, width = home_ref.shape
     depth = weight.shape[0] // blocks
     rank = shrunk_ref.shape[0]
     slots = up_ref.shape[0] // rank
     weight_copies = [
         pltpu.make_async_copy(
-            weight_refs[b].at[pl.ds(0, depth)],
+            weight_refs[spots[b][0]].at[pl.ds(spots[b][1], depth)],
             weight.at[pl.ds(pl.multiple_of(numbers[1 + b] * depth, depth), depth)],
             sems.at[len(layout) + b],
         )
@@ -360,21 +361,22 @@
         for low in range(0, width, HEAD_WIDTH):
             head = total[:, low : low + HEAD_WIDTH]
             turned = head * cosine + pltpu.roll(head, HEAD_WIDTH // 2, 1) * sine
-            out_ref[block, :, low : low + HEAD_WIDTH] = turned.astype(jnp.bfloat16)
-
-
-def project(numbers, layout, normed, weights, shrunk, up, cosine, sine):
+            out_ref = (home_ref, away_ref)[i // 2]
+            out_ref[i % 2, :, low : low + HEAD_WIDTH] = turned.astype(jnp.bfloat16)
+
+
+def project(numbers, layout, spots, normed, weights, shrunk, up, cosine, sine):
     rows, features = normed[0].shape
     width = weights[0].shape[1]
-    blocks = len(weights)
+    blocks = len(spots)
     vmem = pl.BlockSpec(memory_space=pltpu.VMEM)
     return pl.pallas_call(
-        functools.partial(project_kernel, layout, blocks),
-        out_shape=jax.ShapeDtypeStruct((PAIR, rows, width), jnp.bfloat16),
+        functools.partial(project_kernel, layout, spots),
+        out_shape=(jax.ShapeDtypeStruct((PAIR // 2, rows, width), jnp.bfloat16),) * 2,
         in_specs=[pl.BlockSpec(memory_space=pltpu.SMEM)]
-        + [pl.BlockSpec(memory_space=pl.ANY)] * (len(layout) + blocks)
+        + [pl.BlockSpec(memory_space=pl.ANY)] * (len(layout) + len(weights))
         + [vmem] * 4,
-        out_specs=vmem,
+        out_specs=(vmem, vmem),
         scratch_shapes=[
             pltpu.VMEM((PAIR, rows, features), jnp.bfloat16),
             pltpu.VMEM((features, width), jnp.bfloat16),
@@ -386,74 +388,95 @@
     )(numbers, *normed, *weights, shrunk, up, cosine, sine)
 
 
+def largest_square(value):
+    wide = value.astype(jnp.float32)
+    ones = jnp.ones((HEAD_WIDTH, HEAD_WIDTH), jnp.bfloat16)
+    sums = jnp.dot((wide * wide).astype(jnp.bfloat16), ones, preferred_element_type=jnp.float32)
+    return jnp.max(sums, axis=0, keepdims=True)
+
+
+def window_kernel(
+    column, numbers, older_ref, old_ref, own_ref, keys, turned, longest, values, sems
+):
+    rows = own_ref.shape[0] // PAIR
+    value_column = own_ref.shape[1] // 2 + column
+    copies = []
+    for kind, (low, target) in enumerate(((value_column, values), (column, keys))):
+        for b, source in enumerate((older_ref, old_ref, own_ref)):
+            for i in range(PAIR):
+                place = pl.multiple_of(numbers[i] + b * PAIR * rows, rows)
+                copies.append(
+                    pltpu.make_async_copy(
+                        source.at[pl.ds(i * rows, rows), pl.ds(low, HEAD_WIDTH)],
+                        target.at[pl.ds(place, rows)],
+                        sems.at[kind, b * PAIR + i],
+                    )
+                )
+    for copy in copies:
+        copy.start()
+    turned[HEAD_WIDTH:] = jnp.ones(
+        (turned.shape[0] - HEAD_WIDTH, turned.shape[1]), jnp.bfloat16
+    )
+    longest[...] = jnp.zeros(longest.shape, jnp.float32)
+    for copy in copies:
+        copy.wait()
+
+    def turn(i, carry):
+        part = pl.ds(pl.multiple_of(i * KEY_TILE, KEY_TILE), KEY_TILE)
+        turned[:HEAD_WIDTH, part] = values[part].T
+        longest[...] = jnp.maximum(longest[...], largest_square(keys[part]))
+        return carry
+
+    lax.fori_loop(0, keys.shape[0] // KEY_TILE, turn, 0)
+
+
+def window(column, numbers, older, old, own):
+    key_total = 3 * own.shape[0]
+    vmem = pl.BlockSpec(memory_space=pltpu.VMEM)
+    return pl.pallas_call(
+        functools.partial(window_kernel, column),
+        out_shape=(
+            jax.ShapeDtypeStruct((key_total, HEAD_WIDTH), jnp.bfloat16),
+            jax.ShapeDtypeStruct((HEAD_WIDTH + 16, key_total), jnp.bfloat16),
+            jax.ShapeDtypeStruct((1, HEAD_WIDTH), jnp.float32),
+        ),
+        in_specs=[pl.BlockSpec(memory_space=pltpu.SMEM)]
+        + [pl.BlockSpec(memory_space=pl.ANY)] * 3,
+        out_specs=(vmem, vmem, vmem),
+        scratch_shapes=[
+            pltpu.VMEM((key_total, HEAD_WIDTH), jnp.bfloat16),
+            pltpu.SemaphoreType.DMA((2, 3 * PAIR)),
+        ],
+        compiler_params=pltpu.CompilerParams(vmem_limit_bytes=60 * 1024 * 1024),
+        cost_estimate=pl.CostEstimate(flops=1000, bytes_accessed=1000, transcendentals=0),
+        name="window",
+    )(numbers, older, old, own)
+
+
 def attend_kernel(
-    column,
-    numbers,
-    start_ref,
-    query_ref,
-    older_ref,
-    old_ref,
-    own_ref,
-    out_ref,
-    keys,
-    values,
-    turned,
-    total,
-    top_ref,
-    sems,
+    numbers, start_ref, query_ref, keys, turned, longest, out_ref, total, top_ref
 ):
     step = pl.program_id(0)
     tiles = pl.num_programs(0)
-    rows = own_ref.shape[0] // PAIR
-    tile_rows = query_ref.shape[1]
-    group = query_ref.shape[2] // HEAD_WIDTH
-    value_column = own_ref.shape[1] // 2 + column
-
-    @pl.when(step == 0)
-    def _():
-        copies = []
-        for kind, (low, target) in enumerate(((value_column, values), (column, keys))):
-            for b, source in enumerate((older_ref, old_ref, own_ref)):
-                for i in range(PAIR):
-                    place = pl.multiple_of(numbers[2 * tiles + i] + b * PAIR * rows, rows)
-                    copies.append(
-                        pltpu.make_async_copy(
-                            source.at[pl.ds(i * rows, rows), pl.ds(low, HEAD_WIDTH)],
-                            target.at[pl.ds(place, rows)],
-                            sems.at[kind, b * PAIR + i],
-                        )
-                    )
-        for copy in copies:
-            copy.start()
-        ones = turned.shape[0] - HEAD_WIDTH
-        turned[HEAD_WIDTH:] = jnp.ones((ones, turned.shape[1]), jnp.bfloat16)
-        for copy in copies[: len(copies) // 2]:
-            copy.wait()
-
-        def turn(i, carry):
-            low = pl.multiple_of(i * KEY_TILE, KEY_TILE)
-            turned[:HEAD_WIDTH, pl.ds(low, KEY_TILE)] = values[pl.ds(low, KEY_TILE)].T
-            return carry
-
-        lax.fori_loop(0, keys.shape[0] // KEY_TILE, turn, 0)
-        for copy in copies[len(copies) // 2 :]:
-            copy.wait()
-
+    _, tile_rows, width = query_ref.shape
+    group = width // HEAD_WIDTH
     first_token = numbers[step]
     low_start = numbers[tiles + step]
-    base = numbers[2 * tiles + PAIR]
+    base = numbers[2 * tiles]
+    factor = math.log2(math.e) / math.sqrt(HEAD_WIDTH)
     queries = [query_ref[0, :, h * HEAD_WIDTH : (h + 1) * HEAD_WIDTH] for h in range(group)]
-    factor = math.log2(math.e) / math.sqrt(HEAD_WIDTH)
+    bound = functools.reduce(jnp.maximum, [largest_square(part) for part in queries])
+    small = jnp.max(bound * longest[...]) * (factor * factor) < SAFE_POWER * SAFE_POWER
+    total[...] = jnp.zeros(total.shape, jnp.float32)
     top_ref[...] = jnp.full(top_ref.shape, LOWEST, jnp.float32)
-    total[...] = jnp.zeros(total.shape, jnp.float32)
-
-    def one_tile(tile, carry):
+
+    def add(tile, careful):
         low = pl.multiple_of(tile * KEY_TILE, KEY_TILE)
+        here = keys[pl.ds(low, KEY_TILE)]
         shape = (KEY_TILE, tile_rows)
         key_index = base + low + lax.broadcasted_iota(jnp.int32, shape, 0)
         token = first_token + lax.broadcasted_iota(jnp.int32, shape, 1)
         seen = (key_index <= token) & (key_index >= start_ref[0])
-        here = keys[pl.ds(low, KEY_TILE)]
         products = [
             lax.dot_general(
                 here, query, (((1,), (1,)), ((), ())), preferred_element_type=jnp.float32
@@ -461,59 +484,116 @@
             for query in queries
         ]
         for h in range(group):
-            scores = jnp.where(seen, products[h] * factor, LOWEST)
-            old_top = top_ref[h]
-            new_top = jnp.maximum(old_top, jnp.max(scores, axis=0, keepdims=True))
-            expo = jnp.exp2(scores - new_top)
-            top_ref[h] = new_top
-            total[h] = total[h] * jnp.exp2(old_top - new_top) + jnp.dot(
+            power = jnp.where(seen, products[h] * factor, LOWEST)
+            before = total[h]
+            if careful:
+                old_top = top_ref[h]
+                new_top = jnp.maximum(old_top, jnp.max(power, axis=0, keepdims=True))
+                top_ref[h] = new_top
+                power = power - new_top
+                before = before * jnp.exp2(old_top - new_top)
+            total[h] = before + jnp.dot(
                 turned[:, pl.ds(low, KEY_TILE)],
-                expo.astype(jnp.bfloat16),
+                jnp.exp2(power).astype(jnp.bfloat16),
                 preferred_element_type=jnp.float32,
             )
+
+    def plain_tile(tile, carry):
+        add(tile, False)
+        return carry
+
+    def careful_tile(tile, carry):
+        add(tile, True)
         return carry
 
     from_tile = (low_start - base) // KEY_TILE
     to_tile = (first_token + tile_rows - 1 - base) // KEY_TILE + 1
-    lax.fori_loop(from_tile, to_tile, one_tile, 0)
+    middle = jnp.where(small, to_tile, from_tile)
+    lax.fori_loop(from_tile, middle, plain_tile, 0)
+    lax.fori_loop(middle, to_tile, careful_tile, 0)
     for h in range(group):
         mixed = total[h, :HEAD_WIDTH] / total[h, HEAD_WIDTH : HEAD_WIDTH + 1]
         out_ref[0, :, h * HEAD_WIDTH : (h + 1) * HEAD_WIDTH] = mixed.T.astype(jnp.bfloat16)
 
 
-def attend(column, numbers, tile_starts, queries, older, old, own):
+def attend(numbers, tile_starts, queries, keys, turned, longest):
     tiles, tile_rows, width = queries.shape
-    key_total = 3 * own.shape[0]
     group = width // HEAD_WIDTH
-    deep = HEAD_WIDTH + 16
-    anywhere = pl.BlockSpec(memory_space=pl.ANY)
+    deep = turned.shape[0]
+
+    def whole(array):
+        return pl.BlockSpec(array.shape, lambda i, n: (0, 0))
+
     return pl.pallas_call(
-        functools.partial(attend_kernel, column),
+        attend_kernel,
         grid_spec=pltpu.PrefetchScalarGridSpec(
             num_scalar_prefetch=1,
             grid=(tiles,),
             in_specs=[
                 pl.BlockSpec((1, 1, tile_rows), lambda i, n: (i, 0, 0)),
                 pl.BlockSpec((1, tile_rows, width), lambda i, n: (i, 0, 0)),
-                anywhere,
-                anywhere,
-                anywhere,
+                whole(keys),
+                whole(turned),
+                whole(longest),
             ],
             out_specs=pl.BlockSpec((1, tile_rows, width), lambda i, n: (i, 0, 0)),
             scratch_shapes=[
-                pltpu.VMEM((key_total, HEAD_WIDTH), jnp.bfloat16),
-                pltpu.VMEM((key_total, HEAD_WIDTH), jnp.bfloat16),
-                pltpu.VMEM((deep, key_total), jnp.bfloat16),
                 pltpu.VMEM((group, deep, tile_rows), jnp.float32),
                 pltpu.VMEM((group, 1, tile_rows), jnp.float32),
-                pltpu.SemaphoreType.DMA((2, 3 * PAIR)),
             ],
         ),
         out_shape=jax.ShapeDtypeStruct(queries.shape, jnp.bfloat16),
         compiler_params=pltpu.CompilerParams(vmem_limit_bytes=60 * 1024 * 1024),
         cost_estimate=pl.CostEstimate(flops=1000, bytes_accessed=1000, transcendentals=0),
         name="attend",
-    )(numbers, tile_starts, queries, older, old, own)
+    )(numbers, tile_starts, queries, keys, turned, longest)
+
+
+def place_kernel(numbers, *refs):
+    sources, outs, (held, sems, out_sems) = refs[:-5], refs[-5:-3], refs[-3:]
+    width = sources[0].shape[2]
+    each = len(sources) // len(outs)
+    copies = [
+        pltpu.make_async_copy(
+            source.at[numbers[2 * n]],
+            held.at[n // each, :, pl.ds(pl.multiple_of(numbers[2 * n + 1], width), width)],
+            sems.at[n],
+        )
+        for n, source in enumerate(sources)
+    ]
+    for copy in copies:
+        copy.start()
+    last = [
+        pltpu.make_async_copy(held.at[kind], out, out_sems.at[kind])
+        for kind, out in enumerate(outs)
+    ]
+    for kind, whole in enumerate(last):
+        for copy in copies[kind * each : (kind + 1) * each]:
+            copy.wait()
+        whole.start()
+    for whole in last:
+        whole.wait()
+
+
+def place(blocks, columns):
+    numbers = jnp.stack([n for _, index, low in blocks for n in (index, low)]).astype(jnp.int32)
+    arrays = [array for array, _, _ in blocks]
+    _, rows, _ = arrays[0].shape
+    return pl.pallas_call(
+        place_kernel,
+        out_shape=(jax.ShapeDtypeStruct((rows, columns), arrays[0].dtype),) * 2,
+        in_specs=[pl.BlockSpec(memory_space=pltpu.SMEM)]
+        + [pl.BlockSpec(memory_space=pl.ANY)] * len(blocks),
+        out_specs=(pl.BlockSpec(memory_space=pl.ANY),) * 2,
+        scratch_shapes=[
+            pltpu.VMEM((2, rows, columns), arrays[0].dtype),
+            pltpu.SemaphoreType.DMA((len(blocks),)),
+            pltpu.SemaphoreType.DMA((2,)),
+        ],
+        compiler_params=pltpu.CompilerParams(vmem_limit_bytes=60 * 1024 * 1024),
+        cost_estimate=pl.CostEstimate(flops=1000, bytes_accessed=1000, transcendentals=0),
+        name="place",
+    )(numbers, *arrays)
 
 
 def pair_body(
@@ -577,8 +657,9 @@
     from_core = sent["weight c"]
     mine = in_order(core, weight_part(1 - x, core), from_core[wq_rows:])
     kept = in_order(core, weight_part(x, core), from_core[:wq_rows])
-    sent.run([], [("weight x0", mine[:, :chunk], x_swap)])
-    key_value_cache, hidden = sent.tie([key_value_cache, hidden], ["weight x0"])
+    first_mine, key_value_cache = lax.optimization_barrier((mine[:, :chunk], key_value_cache))
+    sent.run([], [("weight x0", first_mine, x_swap)])
+    (hidden,) = sent.tie([hidden], ["weight x0"])
 
     page_count = logical_page_table.shape[1]
     page_rows = rows // page_count
@@ -632,9 +713,7 @@
     sine = jnp.concatenate([-sine, sine], axis=1).reshape(PAIR, rows, HEAD_WIDTH)
 
     chosen = choose(prompt_adapter_index, sent["adapters"].reshape(count, 2 * rank, part), chunk)
-    pieces = [
-        jnp.concatenate([in_order(x, kept[:, :chunk], sent["weight x0"]), chosen], axis=0)
-    ]
+    pieces = [in_order(x, kept[:, :chunk], sent["weight x0"])]
 
     def along_z(g, k):
         return (f"z{g} {k}", pieces[g], functools.partial(shift_z, steps=k))
@@ -679,26 +758,39 @@
         [
             along_z(0, 2),
             along_z(1, 1),
-            along_y(0, 1),
-            along_y(0, 3),
+            ("y0 1 3", jnp.concatenate([sent["z0 1"], sent["z0 3"]], axis=0), y_swap),
             along_y(1, 0),
             normed_part(0),
+        ]
+        + [
+            (f"adapters z{k}", chosen, functools.partial(shift_z, steps=k)) for k in order[1:]
         ],
     )
     cache_own = jnp.concatenate([cache_part(x, core), cache_core[:rows], sent["cache x"]], axis=0)
-    cosine, sine = sent.tie([cosine, sine], ["y0 1"])
+    cosine, sine = sent.tie([cosine, sine], ["y1 0"])
     sent.run(
-        ["z0 2", "z1 1", "y0 1", "y0 3", "y1 0", "normed x0"],
+        ["z0 2", "z1 1", "y0 1 3", "y1 0", "normed x0"]
+        + [f"adapters z{k}" for k in order[1:]],
         [
             ("cache z", cache_own, older),
             along_y(0, 2),
             along_y(1, 1),
             normed_part(1),
             normed_on(0),
-        ],
+            (
+                "adapters y",
+                jnp.concatenate(
+                    [chosen] + [sent[f"adapters z{k}"] for k in order[1:]], axis=0
+                ),
+                y_swap,
+            ),
+        ],
+    )
+    adapters_near = jnp.concatenate(
+        [chosen] + [sent[f"adapters z{k}"] for k in order[1:]], axis=0
     )
     sent.run(
-        ["cache z", "y0 2", "y1 1", "normed x1", "normed xc0"],
+        ["cache z", "y0 2", "y1 1", "normed x1", "normed xc0", "adapters y"],
         [
             normed_on(1),
             along_z(1, 3),
@@ -709,11 +801,6 @@
     normed = [normed_own, sent["normed c"]]
     normed += [sent[f"normed {way}{n}"] for way in ("x", "xc") for n in range(2)]
     layout = ((0, 0), (1, 0)) + tuple((i, cuts[n]) for i in (2, 3) for n in range(2))
-
-    def weights_of(g):
-        return [
-            sent[f"{way}{g} {k}"] if k or way == "y" else pieces[g] for k in order for way in "zy"
-        ]
 
     members = jnp.arange(PAIR, dtype=jnp.int32)
     places = [((z - k) % z_count) * 2 + (y ^ dy) for k in order for dy in (0, 1)]
@@ -726,89 +813,109 @@
             ends,
         ]
     ).astype(jnp.int32)
-    weights0 = weights_of(0)
-    partial, up = shrink(numbers, layout, normed, weights0, wq_depth, part, slots, rank)
+    partial, up = shrink(
+        numbers,
+        layout,
+        normed,
+        adapters_near,
+        sent["adapters y"],
+        2 * z_count,
+        part,
+        slots,
+        rank,
+    )
     partial = partial + swap(partial, 1)
     partial = partial + swap(partial, 2)
     shrunk = partial.astype(jnp.bfloat16)
 
-    def project_part(g, weights, shrunk):
+    def project_part(g, spots, weights, shrunk):
         return project(
-            numbers, layout, normed, weights, shrunk, up[:, g * chunk : (g + 1) * chunk], cosine, sine
+            numbers, layout, spots, normed, weights, shrunk, up[:, g * chunk : (g + 1) * chunk], cosine, sine
         )
 
-    def attend_part(g, queries, from_row, tile_rows):
-        count_rows = queries.shape[0] * queries.shape[1]
-        tiles = count_rows // tile_rows
-        here = lax.dynamic_slice_in_dim(tok_start, from_row, count_rows, 0)
-        here = here.reshape(tiles, 1, tile_rows)
+    block_starts = jnp.stack(
+        [lax.dynamic_slice_in_dim(tok_start, (quarter ^ i) * rows, rows, 0) for i in range(PAIR)]
+    ).reshape(PAIR, 1, rows)
+
+    def attend_part(g, first, queries):
+        tiles = queries.shape[0]
+        here = block_starts[first : first + tiles]
         steps = jnp.concatenate(
             [
-                first_token + from_row + jnp.arange(tiles, dtype=jnp.int32) * tile_rows,
+                first_token + (quarter ^ members[first : first + tiles]) * rows,
                 here[:, 0, 0],
-                (quarter ^ members) * rows,
                 (first_token - 2 * PAIR * rows)[None],
             ]
         ).astype(jnp.int32)
-        return attend(
+        return attend(steps, here, queries, *windows[g])
+
+    def home(name, g, value):
+        from_x = sent[f"{name} x{g}"]
+        from_core = swap(jnp.stack([value[1], from_x[1]]), 1)
+        found = ((0, value, 0), (2, from_x, 0), (1, from_core, 0), (3, from_core, 1))
+        return [
+            (array, jnp.int32(which), (quarter ^ bits) * width + g * chunk)
+            for bits, array, which in found
+        ]
+
+    depth = wq_depth
+    home0, away0 = project_part(
+        0,
+        ((0, 0), (1, 0), (2, 0), (5, 0), (3, 0), (5, depth), (4, 0), (6, 0)),
+        [pieces[0]]
+        + [sent[name] for name in ("y0 0", "z0 1", "z0 3", "z0 2", "y0 1 3", "y0 2")],
+        shrunk,
+    )
+    away0, home0, cache_old = lax.optimization_barrier((away0, home0, sent["cache y"]))
+    windows = [
+        window(
             g * HEAD_WIDTH,
-            steps,
-            here,
-            queries.reshape(tiles, tile_rows, chunk),
+            ((quarter ^ members) * rows).astype(jnp.int32),
             sent["cache z"],
-            sent["cache y"],
+            cache_old,
             cache_own,
-        ).reshape(queries.shape)
-
-    def away(value):
-        return lax.dynamic_slice_in_dim(value, 2 * (1 - x), 2, 0)
-
-    def at_home(value):
-        return lax.dynamic_slice_in_dim(value, 2 * x, 2, 0)
-
-    def home(stay, from_x, g, whole):
-
-        def block(found, which):
-            return lax.dynamic_index_in_dim(found, which, 0, keepdims=False)
-
-        from_core = swap(jnp.stack([block(stay, 1 - core), block(from_x, 1 - core)]), 1)
-        found = (
-            (0, block(stay, core)),
-            (2, block(from_x, core)),
-            (1, from_core[0]),
-            (3, from_core[1]),
         )
-        for bits, piece in found:
-            low = (quarter ^ bits) * width + g * chunk
-            whole = lax.dynamic_update_slice_in_dim(whole, piece, low, 1)
-        return whole
-
-    queries0 = project_part(0, weights0, shrunk)
+        for g in range(kv_heads)
+    ]
+
+    sent.run([], [("queries x0", away0, x_swap)])
+    attended_away0 = attend_part(0, 2, away0)
+    attended_away0, last3, last2 = lax.optimization_barrier(
+        (attended_away0, sent["z1 3"], sent["z1 2"])
+    )
     sent.run(
-        ["cache y", "z1 3", "z1 2"],
-        [along_y(1, 3), along_y(1, 2), ("queries x0", away(queries0), x_swap)],
-    )
-    attended0 = attend_part(0, queries0, 0, PAIR * rows // 3)
-    sent.run([], [("attended x0", away(attended0), x_swap)])
+        ["cache y"],
+        [
+            ("y1 3 2", jnp.concatenate([last3, last2], axis=0), y_swap),
+            ("attended x0", attended_away0, x_swap),
+        ],
+    )
+    attended_home0 = attend_part(0, 0, home0)
+    shrunk, attended_home0, *windows[1] = lax.optimization_barrier(
+        (shrunk, attended_home0, *windows[1])
+    )
     (shrunk,) = sent.tie([shrunk], ["queries x0"])
-    queries1 = project_part(1, weights_of(1), shrunk)
-    queries_away = away(queries1)
-    sent.run([], [("queries x1", queries_away, x_swap)])
-    (queries_away,) = sent.tie([queries_away], ["attended x0"])
-    attended_away = attend_part(1, queries_away, 2 * (1 - x) * rows, rows)
-    sent.run([], [("attended x1", attended_away, x_swap)])
-    (queries_home,) = sent.tie([at_home(queries1)], ["queries x1"])
-    attended1 = attend_part(1, queries_home, 2 * x * rows, rows)
-    outs = []
-    for name, parts in (
-        ("queries", (at_home(queries0), queries_home)),
-        ("attended", (at_home(attended0), attended1)),
-    ):
-        whole = jnp.zeros((rows, q_cols), jnp.bfloat16)
-        for g, stay in enumerate(parts):
-            whole = home(stay, sent[f"{name} x{g}"], g, whole)
-        outs.append(whole)
-    return tuple(outs)
+    home1, away1 = project_part(
+        1,
+        ((0, 0), (1, 0), (2, 0), (5, 0), (3, 0), (6, 0), (4, 0), (6, depth)),
+        [pieces[1]]
+        + [sent[name] for name in ("y1 0", "z1 1", "z1 3", "z1 2", "y1 1", "y1 3 2")],
+        shrunk,
+    )
+    sent.run([], [("queries x1", away1, x_swap)])
+    (away1,) = sent.tie([away1], ["attended x0"])
+    attended_away1 = attend_part(1, 2, away1)
+    sent.run(["queries x1"], [("attended x1", attended_away1, x_swap)])
+    attended_home1 = attend_part(1, 0, home1)
+    return tuple(
+        place(
+            home("queries", 0, home0)
+            + home("queries", 1, home1)
+            + home("attended", 0, attended_home0)
+            + home("attended", 1, attended_home1),
+            q_cols,
+        )
+    )
 
 
 def solution(mesh):

time: 352 us -> 342 us (0.972)
  the two profiles are of different devices: /device:TPU:9 before, /device:TPU:29 now
where the time goes in v2:
time: 342 us; the launch traced here: 336 us
  Pallas kernels  118 us (35%)
  waiting for transfers between devices  98.3 us (29%)
  starting transfers between devices  62.6 us (18%)
  other arithmetic  27.8 us (8%)
  local copies, waits for them, and re-layouts  21.8 us (6%)
  between operations  7.62 us (2%)
    pallas_call x4, Pallas kernels, attend(): pl.pallas_call(attend_kernel, grid_spec=pltpu.PrefetchScalarGridSpec(num_...  65.7 us
    ppermute x28, starting transfers between devices, swap(): return lax.ppermute(value, 'page', [(p, p ^ bit) for p in range(count)])  45.3 us
    ppermute x28, waiting for transfers between devices, swap(): return lax.ppermute(value, 'page', [(p, p ^ bit) for p in range(count)])  44.5 us
    ppermute x1, waiting for transfers between devices, older(): return lax.ppermute(value, 'page', [(p, p + 8) for p in range(count - 8)])  40.2 us
    pallas_call x2, Pallas kernels, project(): pl.pallas_call(functools.partial(project_kernel, layout, spots), out_shap...  28.5 us
    ppermute x9, waiting for transfers between devices, shift_z(): lax.ppermute(value, 'page', [(p, (p + 8 * steps) % count) for p in range(...  13.5 us
    pallas_call x2, Pallas kernels, window(): pl.pallas_call(functools.partial(window_kernel, column), out_shape=(jax.S...  11.6 us
    ppermute x9, starting transfers between devices, shift_z(): lax.ppermute(value, 'page', [(p, (p + 8 * steps) % count) for p in range(...  10.2 us
  transfers between devices with their start and end apart: 39, of which 12 were waited for; matrix products, arithmetic and copies ran while one was open for 12% of the time, Pallas kernels for 34%

profile of v2, /device:TPU:29, one launch (start us, length us, event | category | flops | bytes accessed | tf_op | source)
XLA Modules:
  0.0 336.5 jit_solution(1868658045530090796)
XLA Ops:
  0.7 1.3 constant_dynamic-slice_fusion.11
  3.8 5.6 %all-to-all-start = ((bf16[32,32,128]{2,1,0:T(8,128)(2,1)}), bf16[32,32,128]{2,1,0:T(8,128)(2,1)S(1)}, u32[]{:S(2)}, u32[]{:S(2)}) async-start(bf16[32,32,128]{2,1,0:T(8,128)(2,1)} %bitcast.21), calls=%async_computation | async-start | bytes 524288 | tf_op jit(solution)/shard_map/all_to_all | solution.py:644
  15.7 1.3 maximum_select_fusion
  20.4 4.9 %collective-permute-done.1 = bf16[256,512]{1,0:T(8,128)(2,1)} collective-permute-done((bf16[256,512]{1,0:T(8,128)(2,1)S(1)}, bf16[256,512]{1,0:T(8,128)(2,1)}, u32[]{:S(2)}, u32[]{:S(2)}) %collective-permute-start.1) | collective-permute-done | bytes 262176 | tf_op jit(solution)/shard_map/ppermute | solution.py:156
  31.8 2.2 choose.1
  36.4 1.3 collective-permute-start.2
  37.9 3.0 collective-permute-start.3
  42.5 1.8 collective-permute-done.2
  45.4 1.9 fusion.8
  48.4 4.2 %collective-permute-done.4.refs_9_ = bf16[512,512]{1,0:T(8,128)(2,1)S(1)} collective-permute-done((bf16[512,512]{1,0:T(8,128)(2,1)S(1)}, bf16[512,512]{1,0:T(8,128)(2,1)S(1)}, u32[]{:S(2)}, u32[]{:S(2)}) %collective-permute-start.4) | collective-permute-done | bytes 524320 | tf_op jit(solution)/shard_map/ppermute | solution.py:161
  52.6 9.3 %collective-permute-done.3.refs_8_ = bf16[512,512]{1,0:T(8,128)(2,1)S(1)} collective-permute-done((bf16[512,512]{1,0:T(8,128)(2,1)S(1)}, bf16[512,512]{1,0:T(8,128)(2,1)S(1)}, u32[]{:S(2)}, u32[]{:S(2)}) %collective-permute-start.3) | collective-permute-done | bytes 524320 | tf_op jit(solution)/shard_map/ppermute | solution.py:161
  65.5 2.1 collective-permute-start.14
  67.7 3.1 collective-permute-start.12
  70.8 2.8 fusion.7
  75.4 1.7 pad_maximum_fusion.4
  77.1 1.3 pad_maximum_fusion.own_ref
  79.1 20.0 %collective-permute-done.16.refs_7_ = bf16[512,512]{1,0:T(8,128)(2,1)S(1)} collective-permute-done((bf16[512,512]{1,0:T(8,128)(2,1)}, bf16[512,512]{1,0:T(8,128)(2,1)S(1)}, u32[]{:S(2)}, u32[]{:S(2)}) %collective-permute-start.16) | collective-permute-done | bytes 524320 | tf_op jit(solution)/shard_map/ppermute | solution.py:156
  99.2 1.5 collective-permute-start.18
  100.7 1.4 collective-permute-start.17
  102.1 3.1 collective-permute-start.21
  106.7 40.2 %collective-permute-done.18.older_ref = bf16[1536,512]{1,0:T(8,128)(2,1)} collective-permute-done((bf16[1536,512]{1,0:T(8,128)(2,1)}, bf16[1536,512]{1,0:T(8,128)(2,1)}, u32[]{:S(2)}, u32[]{:S(2)}) %collective-permute-start.18) | collective-permute-done | bytes 1572896 | tf_op jit(solution)/shard_map/ppermute | solution.py:725
  148.1 3.3 broadcast_select_fusion
  151.5 2.6 collective-permute-done.22.refs_7_
  155.1 1.8 collective-permute-start.23
  157.0 1.3 collective-permute-start.26
  158.3 1.3 concatenate.94.numbers
  160.4 1.7 fusion.6.refs_6_
  163.2 4.9 %shrink.1 = (f32[16,1536]{1,0:T(8,128)}, bf16[128,1024]{1,0:T(8,128)(2,1)}) custom-call(s32[29]{0:T(128)} %concatenate.94.numbers, bf16[384,4096]{1,0:T(8,128)(2,1)} %copy-done, bf16[384,4096]{1,0:T(8,128)(2,1)} %collective-permute-done.8.refs_1_, bf16[192,4096]{1,0:T(8,128)(2,1)} %copy-done.1, bf16[192,4096]{1,0:T(8,128)(2,1)} %copy-done.2, ...), custom_call_target="tpu_custom_call" | custom-call | flops 1000 | bytes 1000 | tf_op jit(solution)/shard_map/shrink/pallas_call | solution.py:296
  172.2 1.7 fusion.13
  173.9 1.3 collective-permute-done.25
  175.8 14.2 %project.2 = (bf16[2,384,512]{2,1,0:T(8,128)(2,1)}, bf16[2,384,512]{2,1,0:T(8,128)(2,1)}) custom-call(s32[29]{0:T(128)} %concatenate.94.numbers, bf16[384,4096]{1,0:T(8,128)(2,1)} %copy-done, bf16[384,4096]{1,0:T(8,128)(2,1)} %collective-permute-done.8.refs_1_, bf16[192,4096]{1,0:T(8,128)(2,1)} %copy-done.1, bf16[192,4096]{1,0:T(8,128)(2,1)} %copy-done.2, ...), custom_call_target="tpu_custom_call" | custom-call | flops 1000 | bytes 1000 | tf_op jit(solution)/shard_map/project/pallas_call | solution.py:373
  190.0 3.4 %collective-permute-done.26.old_ref = bf16[1536,512]{1,0:T(8,128)(2,1)} collective-permute-done((bf16[1536,512]{1,0:T(8,128)(2,1)}, bf16[1536,512]{1,0:T(8,128)(2,1)}, u32[]{:S(2)}, u32[]{:S(2)}) %collective-permute-start.26) | collective-permute-done | bytes 1572896 | tf_op jit(solution)/shard_map/ppermute | solution.py:156
  193.4 5.8 %window.2 = (bf16[4608,128]{1,0:T(8,128)(2,1)}, bf16[144,4608]{1,0:T(8,128)(2,1)}, f32[1,128]{1,0:T(1,128)}) custom-call(s32[4]{0:T(128)} %xor_multiply_fusion.numbers, bf16[1536,512]{1,0:T(8,128)(2,1)} %collective-permute-done.18.older_ref, bf16[1536,512]{1,0:T(8,128)(2,1)} %collective-permute-done.26.old_ref, bf16[1536,512]{1,0:T(8,128)(2,1)} %pad_maximum_fusion.own_ref), custom_call_target="tpu_custom_call" | custom-call | flops 1000 | bytes 1000 | tf_op jit(solution)/shard_map/window/pallas_call | solution.py:436
  199.2 10.0 %attend.5 = bf16[2,384,512]{2,1,0:T(8,128)(2,1)} custom-call(s32[5]{0:T(128)} %add_add_fusion.1.numbers, s32[2,1,384]{2,1,0:T(1,128)} %copy-done.44, bf16[2,384,512]{2,1,0:T(8,128)(2,1)} %get-tuple-element.137.query_ref, bf16[4608,128]{1,0:T(8,128)(2,1)} %get-tuple-element.130.keys, bf16[144,4608]{1,0:T(8,128)(2,1)} %get-tuple-element.131.turned, ...), custom_call_target="tpu_custom_call" | custom-call | flops 1000 | bytes 1000 | tf_op jit(solution)/shard_map/attend/pallas_call | solution.py:527
  210.3 9.6 %collective-permute-start.31 = (bf16[1024,512]{1,0:T(8,128)(2,1)}, bf16[1024,512]{1,0:T(8,128)(2,1)}, u32[]{:S(2)}, u32[]{:S(2)}) collective-permute-start(bf16[1024,512]{1,0:T(8,128)(2,1)} %pad_maximum_fusion.2), channel_id=1, source_target_pairs={{0,4},{1,5},{2,6},{3,7},{4,0},{5,1},{6,2},{7,3},{8,12},{9,13},{10,... | collective-permute-start | bytes 3145736 | tf_op jit(solution)/shard_map/ppermute | solution.py:156
  219.9 4.5 %collective-permute-start.27 = (bf16[2,384,512]{2,1,0:T(8,128)(2,1)S(1)}, bf16[2,384,512]{2,1,0:T(8,128)(2,1)S(1)}, u32[]{:S(2)}, u32[]{:S(2)}) collective-permute-start(bf16[2,384,512]{2,1,0:T(8,128)(2,1)S(1)} %copy-done.27), channel_id=1, source_target_pairs={{0,2},{1,3},{2,0},{3,1},{4,6},{5,7},{6,4},{7,5},{8,10},{9,11},{10,... | collective-permute-start | bytes 2359304 | tf_op jit(solution)/shard_map/ppermute | solution.py:156
  225.3 5.8 %window.3 = (bf16[4608,128]{1,0:T(8,128)(2,1)}, bf16[144,4608]{1,0:T(8,128)(2,1)}, f32[1,128]{1,0:T(1,128)}) custom-call(s32[4]{0:T(128)} %xor_multiply_fusion.numbers, bf16[1536,512]{1,0:T(8,128)(2,1)} %collective-permute-done.18.older_ref, bf16[1536,512]{1,0:T(8,128)(2,1)} %collective-permute-done.26.old_ref, bf16[1536,512]{1,0:T(8,128)(2,1)} %pad_maximum_fusion.own_ref), custom_call_target="tpu_custom_call" | custom-call | flops 1000 | bytes 1000 | tf_op jit(solution)/shard_map/window/pallas_call | solution.py:436
  231.1 22.6 %attend.4.refs_8_ = bf16[2,384,512]{2,1,0:T(8,128)(2,1)} custom-call(s32[5]{0:T(128)} %add_add_fusion.numbers, s32[2,1,384]{2,1,0:T(1,128)} %copy-done.45, bf16[2,384,512]{2,1,0:T(8,128)(2,1)} %get-tuple-element.127.query_ref.refs_0_, bf16[4608,128]{1,0:T(8,128)(2,1)} %get-tuple-element.130.keys, bf16[144,4608]{1,0:T(8,128)(2,1)} %get-tuple-element.131.turned, ...), custom_call_target="tpu_custom_call" | custom-call | flops 1000 | bytes 1000 | tf_op jit(solution)/shard_map/attend/pallas_call | solution.py:527
  253.7 14.4 %project.3 = (bf16[2,384,512]{2,1,0:T(8,128)(2,1)}, bf16[2,384,512]{2,1,0:T(8,128)(2,1)}) custom-call(s32[29]{0:T(128)} %concatenate.94.numbers, bf16[384,4096]{1,0:T(8,128)(2,1)} %copy-done, bf16[384,4096]{1,0:T(8,128)(2,1)} %collective-permute-done.8.refs_1_, bf16[192,4096]{1,0:T(8,128)(2,1)} %copy-done.1, bf16[192,4096]{1,0:T(8,128)(2,1)} %copy-done.2, ...), custom_call_target="tpu_custom_call" | custom-call | flops 1000 | bytes 1000 | tf_op jit(solution)/shard_map/project/pallas_call | solution.py:373
  268.1 1.5 collective-permute-start.33
  269.7 2.2 collective-permute-done.32.refs_9_
  271.9 10.3 %attend.6 = bf16[2,384,512]{2,1,0:T(8,128)(2,1)} custom-call(s32[5]{0:T(128)} %add_add_fusion.1.numbers, s32[2,1,384]{2,1,0:T(1,128)} %copy-done.44, bf16[2,384,512]{2,1,0:T(8,128)(2,1)} %get-tuple-element.152.query_ref, bf16[4608,128]{1,0:T(8,128)(2,1)} %get-tuple-element.153.keys, bf16[144,4608]{1,0:T(8,128)(2,1)} %get-tuple-element.154.turned, ...), custom_call_target="tpu_custom_call" | custom-call | flops 1000 | bytes 1000 | tf_op jit(solution)/shard_map/attend/pallas_call | solution.py:527
  282.2 6.5 %collective-permute-done.33.refs_5_ = bf16[2,384,512]{2,1,0:T(8,128)(2,1)S(1)} collective-permute-done((bf16[2,384,512]{2,1,0:T(8,128)(2,1)}, bf16[2,384,512]{2,1,0:T(8,128)(2,1)S(1)}, u32[]{:S(2)}, u32[]{:S(2)}) %collective-permute-start.33) | collective-permute-done | bytes 786464 | tf_op jit(solution)/shard_map/ppermute | solution.py:156
  288.7 6.4 %collective-permute-start.36 = (bf16[2,384,512]{2,1,0:T(8,128)(2,1)}, bf16[2,384,512]{2,1,0:T(8,128)(2,1)}, u32[]{:S(2)}, u32[]{:S(2)}) collective-permute-start(bf16[2,384,512]{2,1,0:T(8,128)(2,1)} %attend.6), channel_id=1, source_target_pairs={{0,2},{1,3},{2,0},{3,1},{4,6},{5,7},{6,4},{7,5},{8,10},{9,11},{10,... | collective-permute-start | bytes 2359304 | tf_op jit(solution)/shard_map/ppermute | solution.py:156
  296.1 2.9 collective-permute-start.28
  299.1 22.7 %attend.7.refs_12_ = bf16[2,384,512]{2,1,0:T(8,128)(2,1)} custom-call(s32[5]{0:T(128)} %add_add_fusion.numbers, s32[2,1,384]{2,1,0:T(1,128)} %copy-done.45, bf16[2,384,512]{2,1,0:T(8,128)(2,1)} %get-tuple-element.149.query_ref.refs_4_, bf16[4608,128]{1,0:T(8,128)(2,1)} %get-tuple-element.153.keys, bf16[144,4608]{1,0:T(8,128)(2,1)} %get-tuple-element.154.turned, ...), custom_call_target="tpu_custom_call" | custom-call | flops 1000 | bytes 1000 | tf_op jit(solution)/shard_map/attend/pallas_call | solution.py:527
  327.9 1.8 collective-permute-done.37.refs_14_.refs_15_
  330.6 5.4 %place.1 = (bf16[384,4096]{1,0:T(8,128)(2,1)}, bf16[384,4096]{1,0:T(8,128)(2,1)}) custom-call(s32[32]{0:T(128)} %stack.96.numbers, bf16[2,384,512]{2,1,0:T(8,128)(2,1)} %get-tuple-element.127.query_ref.refs_0_, bf16[2,384,512]{2,1,0:T(8,128)(2,1)} %copy-done.21, bf16[2,384,512]{2,1,0:T(8,128)(2,1)} %copy-done.7, bf16[2,384,512]{2,1,0:T(8,128)(2,1)} %copy-done.7, ...), custom_call_target="tpu_custom_call" | custom-call | flops 1000 | bytes 1000 | tf_op jit(solution)/shard_map/place/pallas_call | solution.py:582
  (224 shorter events, 45.0 us)
Async XLA Ops:
  2.1 13.5 %collective-permute-start = (bf16[256,1024]{1,0:T(8,128)(2,1)S(1)}, bf16[256,1024]{1,0:T(8,128)(2,1)S(1)}, u32[]{:S(2)}, u32[]{:S(2)}) collective-permute-start(bf16[256,1024]{1,0:T(8,128)(2,1)S(1)} %pad_maximum_fusion.10), channel_id=1, source_target_pairs={{0,1},{1,0},{2,3},{3,2},{4,5},{5,4},{6,7},{7,6},{8,9},{9,8},{10,11... | collective-permute-start | bytes 1572872 | tf_op jit(solution)/shard_map/ppermute | solution.py:156
  3.8 27.3 %all-to-all-start = ((bf16[32,32,128]{2,1,0:T(8,128)(2,1)}), bf16[32,32,128]{2,1,0:T(8,128)(2,1)S(1)}, u32[]{:S(2)}, u32[]{:S(2)}) async-start(bf16[32,32,128]{2,1,0:T(8,128)(2,1)} %bitcast.21), calls=%async_computation | async-start | bytes 524288 | tf_op jit(solution)/shard_map/all_to_all | solution.py:644
  17.7 7.6 %collective-permute-start.1 = (bf16[256,512]{1,0:T(8,128)(2,1)S(1)}, bf16[256,512]{1,0:T(8,128)(2,1)}, u32[]{:S(2)}, u32[]{:S(2)}) collective-permute-start(bf16[256,512]{1,0:T(8,128)(2,1)S(1)} %get-tuple-element.81), channel_id=1, source_target_pairs={{0,2},{1,3},{2,0},{3,1},{4,6},{5,7},{6,4},{7,5},{8,10},{9,11},{10,... | collective-permute-start | bytes 786440 | tf_op jit(solution)/shard_map/ppermute | solution.py:156
  27.2 35.8 %collective-permute-start.8 = (bf16[384,4096]{1,0:T(8,128)(2,1)S(1)}, bf16[384,4096]{1,0:T(8,128)(2,1)}, u32[]{:S(2)}, u32[]{:S(2)}) collective-permute-start(bf16[384,4096]{1,0:T(8,128)(2,1)S(1)} %fusion.2.refs_0_), channel_id=1, source_target_pairs={{0,1},{1,0},{2,3},{3,2},{4,5},{5,4},{6,7},{7,6},{8,9},{9,8},{10,11... | collective-permute-start | bytes 9437192 | tf_op jit(solution)/shard_map/ppermute | solution.py:156
  30.6 10.4 %collective-permute-start.6 = (bf16[768,512]{1,0:T(8,128)(2,1)}, bf16[768,512]{1,0:T(8,128)(2,1)}, u32[]{:S(2)}, u32[]{:S(2)}) collective-permute-start(bf16[768,512]{1,0:T(8,128)(2,1)} %maximum_maximum_fusion), channel_id=1, source_target_pairs={{0,1},{1,0},{2,3},{3,2},{4,5},{5,4},{6,7},{7,6},{8,9},{9,8},{10,11... | collective-permute-start | bytes 2359304 | tf_op jit(solution)/shard_map/ppermute | solution.py:156
  31.1 33.3 %copy-start.48 = (s32[8,1]{0,1:T(1,128)}, s32[8,1]{0,1:T(1,128)S(1)}, u32[]{:S(2)}) copy-start(s32[8,1]{0,1:T(1,128)S(1)} %reduce-window.8) | copy-start | bytes 100
  36.4 7.8 %collective-permute-start.2 = (bf16[256,512]{1,0:T(8,128)(2,1)S(1)}, bf16[256,512]{1,0:T(8,128)(2,1)S(1)}, u32[]{:S(2)}, u32[]{:S(2)}) collective-permute-start(bf16[256,512]{1,0:T(8,128)(2,1)S(1)} %copy-done.38), channel_id=1, source_target_pairs={{0,2},{1,3},{2,0},{3,1},{4,6},{5,7},{6,4},{7,5},{8,10},{9,11},{10,... | collective-permute-start | bytes 786440 | tf_op jit(solution)/shard_map/ppermute | solution.py:156
  37.7 14.9 %collective-permute-start.4 = (bf16[512,512]{1,0:T(8,128)(2,1)S(1)}, bf16[512,512]{1,0:T(8,128)(2,1)S(1)}, u32[]{:S(2)}, u32[]{:S(2)}) collective-permute-start(bf16[512,512]{1,0:T(8,128)(2,1)S(1)} %maximum_select_fusion.2.refs_6_), channel_id=1, source_target_pairs={{0,24},{1,25},{2,26},{3,27},{4,28},{5,29},{6,30},{7,31},{8,0},{9,1... | collective-permute-start | bytes 1572872 | tf_op jit(solution)/shard_map/ppermute | solution.py:161
  37.9 24.0 %collective-permute-start.3 = (bf16[512,512]{1,0:T(8,128)(2,1)S(1)}, bf16[512,512]{1,0:T(8,128)(2,1)S(1)}, u32[]{:S(2)}, u32[]{:S(2)}) collective-permute-start(bf16[512,512]{1,0:T(8,128)(2,1)S(1)} %maximum_select_fusion.2.refs_6_), channel_id=1, source_target_pairs={{0,8},{1,9},{2,10},{3,11},{4,12},{5,13},{6,14},{7,15},{8,16},{9,17... | collective-permute-start | bytes 1572872 | tf_op jit(solution)/shard_map/ppermute | solution.py:161
  40.9 22.1 %collective-permute-start.5 = (bf16[512,512]{1,0:T(8,128)(2,1)S(1)}, bf16[512,512]{1,0:T(8,128)(2,1)S(1)}, u32[]{:S(2)}, u32[]{:S(2)}) collective-permute-start(bf16[512,512]{1,0:T(8,128)(2,1)S(1)} %maximum_select_fusion.2.refs_6_), channel_id=1, source_target_pairs={{0,4},{1,5},{2,6},{3,7},{4,0},{5,1},{6,2},{7,3},{8,12},{9,13},{10,... | collective-permute-start | bytes 1572872 | tf_op jit(solution)/shard_map/ppermute | solution.py:156
  44.2 18.8 %collective-permute-start.7 = (bf16[768,512]{1,0:T(8,128)(2,1)S(1)}, bf16[768,512]{1,0:T(8,128)(2,1)S(1)}, u32[]{:S(2)}, u32[]{:S(2)}) collective-permute-start(bf16[768,512]{1,0:T(8,128)(2,1)S(1)} %pad_maximum_fusion.3), channel_id=1, source_target_pairs={{0,2},{1,3},{2,0},{3,1},{4,6},{5,7},{6,4},{7,5},{8,10},{9,11},{10,... | collective-permute-start | bytes 2359304 | tf_op jit(solution)/shard_map/ppermute | solution.py:156
  63.9 35.2 %collective-permute-start.11 = (bf16[192,4096]{1,0:T(8,128)(2,1)}, bf16[192,4096]{1,0:T(8,128)(2,1)S(1)}, u32[]{:S(2)}, u32[]{:S(2)}) collective-permute-start(bf16[192,4096]{1,0:T(8,128)(2,1)} %get-tuple-element.93), channel_id=1, source_target_pairs={{0,2},{1,3},{2,0},{3,1},{4,6},{5,7},{6,4},{7,5},{8,10},{9,11},{10,... | collective-permute-start | bytes 4718600 | tf_op jit(solution)/shard_map/ppermute | solution.py:156
  65.1 34.0 %collective-permute-start.15 = (bf16[1024,512]{1,0:T(8,128)(2,1)}, bf16[1024,512]{1,0:T(8,128)(2,1)S(1)}, u32[]{:S(2)}, u32[]{:S(2)}) collective-permute-start(bf16[1024,512]{1,0:T(8,128)(2,1)} %pad_maximum_fusion.1), channel_id=1, source_target_pairs={{0,4},{1,5},{2,6},{3,7},{4,0},{5,1},{6,2},{7,3},{8,12},{9,13},{10,... | collective-permute-start | bytes 3145736 | tf_op jit(solution)/shard_map/ppermute | solution.py:156
  65.5 8.1 %collective-permute-start.14 = (bf16[64,512]{1,0:T(8,128)(2,1)}, bf16[64,512]{1,0:T(8,128)(2,1)S(1)}, u32[]{:S(2)}, u32[]{:S(2)}) collective-permute-start(bf16[64,512]{1,0:T(8,128)(2,1)} %choose.1), channel_id=1, source_target_pairs={{0,16},{1,17},{2,18},{3,19},{4,20},{5,21},{6,22},{7,23},{8,24},{9,... | collective-permute-start | bytes 196616 | tf_op jit(solution)/shard_map/ppermute | solution.py:161
  67.5 6.2 %collective-permute-start.13 = (bf16[64,512]{1,0:T(8,128)(2,1)}, bf16[64,512]{1,0:T(8,128)(2,1)S(1)}, u32[]{:S(2)}, u32[]{:S(2)}) collective-permute-start(bf16[64,512]{1,0:T(8,128)(2,1)} %choose.1), channel_id=1, source_target_pairs={{0,24},{1,25},{2,26},{3,27},{4,28},{5,29},{6,30},{7,31},{8,0},{9,1... | collective-permute-start | bytes 196616 | tf_op jit(solution)/shard_map/ppermute | solution.py:161
  67.7 6.5 %collective-permute-start.12 = (bf16[64,512]{1,0:T(8,128)(2,1)}, bf16[64,512]{1,0:T(8,128)(2,1)S(1)}, u32[]{:S(2)}, u32[]{:S(2)}) collective-permute-start(bf16[64,512]{1,0:T(8,128)(2,1)} %choose.1), channel_id=1, source_target_pairs={{0,8},{1,9},{2,10},{3,11},{4,12},{5,13},{6,14},{7,15},{8,16},{9,17... | collective-permute-start | bytes 196616 | tf_op jit(solution)/shard_map/ppermute | solution.py:161
  73.6 25.5 %collective-permute-start.9 = (bf16[512,512]{1,0:T(8,128)(2,1)}, bf16[512,512]{1,0:T(8,128)(2,1)S(1)}, u32[]{:S(2)}, u32[]{:S(2)}) collective-permute-start(bf16[512,512]{1,0:T(8,128)(2,1)} %copy-done.14), channel_id=1, source_target_pairs={{0,16},{1,17},{2,18},{3,19},{4,20},{5,21},{6,22},{7,23},{8,24},{9,... | collective-permute-start | bytes 1572872 | tf_op jit(solution)/shard_map/ppermute | solution.py:161
  73.7 25.4 %collective-permute-start.10 = (bf16[512,512]{1,0:T(8,128)(2,1)}, bf16[512,512]{1,0:T(8,128)(2,1)S(1)}, u32[]{:S(2)}, u32[]{:S(2)}) collective-permute-start(bf16[512,512]{1,0:T(8,128)(2,1)} %maximum_select_fusion.3.refs_6_), channel_id=1, source_target_pairs={{0,8},{1,9},{2,10},{3,11},{4,12},{5,13},{6,14},{7,15},{8,16},{9,17... | collective-permute-start | bytes 1572872 | tf_op jit(solution)/shard_map/ppermute | solution.py:161
  74.2 25.0 %collective-permute-start.16 = (bf16[512,512]{1,0:T(8,128)(2,1)}, bf16[512,512]{1,0:T(8,128)(2,1)S(1)}, u32[]{:S(2)}, u32[]{:S(2)}) collective-permute-start(bf16[512,512]{1,0:T(8,128)(2,1)} %maximum_select_fusion.3.refs_6_), channel_id=1, source_target_pairs={{0,4},{1,5},{2,6},{3,7},{4,0},{5,1},{6,2},{7,3},{8,12},{9,13},{10,... | collective-permute-start | bytes 1572872 | tf_op jit(solution)/shard_map/ppermute | solution.py:156
  99.2 52.3 %copy-start.1 = (bf16[192,4096]{1,0:T(8,128)(2,1)}, bf16[192,4096]{1,0:T(8,128)(2,1)S(1)}, u32[]{:S(2)}) copy-start(bf16[192,4096]{1,0:T(8,128)(2,1)S(1)} %collective-permute-done.11.refs_2_) | copy-start | bytes 4718596
  99.2 47.7 %collective-permute-start.18 = (bf16[1536,512]{1,0:T(8,128)(2,1)}, bf16[1536,512]{1,0:T(8,128)(2,1)}, u32[]{:S(2)}, u32[]{:S(2)}) collective-permute-start(bf16[1536,512]{1,0:T(8,128)(2,1)} %pad_maximum_fusion.own_ref), channel_id=1, source_target_pairs={{0,8},{1,9},{2,10},{3,11},{4,12},{5,13},{6,14},{7,15},{8,16},{9,17... | collective-permute-start | bytes 4718600 | tf_op jit(solution)/shard_map/ppermute | solution.py:725
  100.7 53.4 %collective-permute-start.17 = (bf16[192,4096]{1,0:T(8,128)(2,1)}, bf16[192,4096]{1,0:T(8,128)(2,1)S(1)}, u32[]{:S(2)}, u32[]{:S(2)}) collective-permute-start(bf16[192,4096]{1,0:T(8,128)(2,1)} %get-tuple-element.101), channel_id=1, source_target_pairs={{0,2},{1,3},{2,0},{3,1},{4,6},{5,7},{6,4},{7,5},{8,10},{9,11},{10,... | collective-permute-start | bytes 4718600 | tf_op jit(solution)/shard_map/ppermute | solution.py:156
  102.1 52.0 %collective-permute-start.21 = (bf16[192,4096]{1,0:T(8,128)(2,1)S(1)}, bf16[192,4096]{1,0:T(8,128)(2,1)}, u32[]{:S(2)}, u32[]{:S(2)}) collective-permute-start(bf16[192,4096]{1,0:T(8,128)(2,1)S(1)} %collective-permute-done.11.refs_2_), channel_id=1, source_target_pairs={{0,1},{1,0},{2,3},{3,2},{4,5},{5,4},{6,7},{7,6},{8,9},{9,8},{10,11... | collective-permute-start | bytes 4718600 | tf_op jit(solution)/shard_map/ppermute | solution.py:156
  105.2 48.8 %collective-permute-start.19 = (bf16[512,512]{1,0:T(8,128)(2,1)}, bf16[512,512]{1,0:T(8,128)(2,1)S(1)}, u32[]{:S(2)}, u32[]{:S(2)}) collective-permute-start(bf16[512,512]{1,0:T(8,128)(2,1)} %copy-done.34), channel_id=1, source_target_pairs={{0,4},{1,5},{2,6},{3,7},{4,0},{5,1},{6,2},{7,3},{8,12},{9,13},{10,... | collective-permute-start | bytes 1572872 | tf_op jit(solution)/shard_map/ppermute | solution.py:156
  105.5 48.6 %collective-permute-start.20 = (bf16[512,512]{1,0:T(8,128)(2,1)}, bf16[512,512]{1,0:T(8,128)(2,1)S(1)}, u32[]{:S(2)}, u32[]{:S(2)}) collective-permute-start(bf16[512,512]{1,0:T(8,128)(2,1)} %copy-done.32), channel_id=1, source_target_pairs={{0,4},{1,5},{2,6},{3,7},{4,0},{5,1},{6,2},{7,3},{8,12},{9,13},{10,... | collective-permute-start | bytes 1572872 | tf_op jit(solution)/shard_map/ppermute | solution.py:156
  146.9 7.1 %collective-permute-start.22 = (bf16[256,512]{1,0:T(8,128)(2,1)}, bf16[256,512]{1,0:T(8,128)(2,1)S(1)}, u32[]{:S(2)}, u32[]{:S(2)}) collective-permute-start(bf16[256,512]{1,0:T(8,128)(2,1)} %fusion.4), channel_id=1, source_target_pairs={{0,4},{1,5},{2,6},{3,7},{4,0},{5,1},{6,2},{7,3},{8,12},{9,13},{10,... | collective-permute-start | bytes 786440 | tf_op jit(solution)/shard_map/ppermute | solution.py:156
  155.1 7.0 %collective-permute-start.23 = (bf16[192,4096]{1,0:T(8,128)(2,1)S(1)}, bf16[192,4096]{1,0:T(8,128)(2,1)S(1)}, u32[]{:S(2)}, u32[]{:S(2)}) collective-permute-start(bf16[192,4096]{1,0:T(8,128)(2,1)S(1)} %collective-permute-done.17.refs_3_), channel_id=1, source_target_pairs={{0,1},{1,0},{2,3},{3,2},{4,5},{5,4},{6,7},{7,6},{8,9},{9,8},{10,11... | collective-permute-start | bytes 4718600 | tf_op jit(solution)/shard_map/ppermute | solution.py:156
  157.0 36.4 %collective-permute-start.26 = (bf16[1536,512]{1,0:T(8,128)(2,1)}, bf16[1536,512]{1,0:T(8,128)(2,1)}, u32[]{:S(2)}, u32[]{:S(2)}) collective-permute-start(bf16[1536,512]{1,0:T(8,128)(2,1)} %broadcast_select_fusion), channel_id=1, source_target_pairs={{0,4},{1,5},{2,6},{3,7},{4,0},{5,1},{6,2},{7,3},{8,12},{9,13},{10,... | collective-permute-start | bytes 4718600 | tf_op jit(solution)/shard_map/ppermute | solution.py:156
  168.1 2.2 collective-permute-start.24
  169.1 40.1 %collective-permute-start.29 = (bf16[512,512]{1,0:T(8,128)(2,1)S(1)}, bf16[512,512]{1,0:T(8,128)(2,1)S(1)}, u32[]{:S(2)}, u32[]{:S(2)}) collective-permute-start(bf16[512,512]{1,0:T(8,128)(2,1)S(1)} %copy-done.13), channel_id=1, source_target_pairs={{0,24},{1,25},{2,26},{3,27},{4,28},{5,29},{6,30},{7,31},{8,0},{9,1... | collective-permute-start | bytes 1572872 | tf_op jit(solution)/shard_map/ppermute | solution.py:161
  170.3 39.0 %collective-permute-start.30 = (bf16[512,512]{1,0:T(8,128)(2,1)S(1)}, bf16[512,512]{1,0:T(8,128)(2,1)S(1)}, u32[]{:S(2)}, u32[]{:S(2)}) collective-permute-start(bf16[512,512]{1,0:T(8,128)(2,1)S(1)} %copy-done.13), channel_id=1, source_target_pairs={{0,16},{1,17},{2,18},{3,19},{4,20},{5,21},{6,22},{7,23},{8,24},{9,... | collective-permute-start | bytes 1572872 | tf_op jit(solution)/shard_map/ppermute | solution.py:161
  171.2 4.0 %collective-permute-start.25 = (f32[16,1536]{1,0:T(8,128)S(1)}, f32[16,1536]{1,0:T(8,128)S(1)}, u32[]{:S(2)}, u32[]{:S(2)}) collective-permute-start(f32[16,1536]{1,0:T(8,128)S(1)} %add.277), channel_id=1, source_target_pairs={{0,2},{1,3},{2,0},{3,1},{4,6},{5,7},{6,4},{7,5},{8,10},{9,11},{10,... | collective-permute-start | bytes 294920 | tf_op jit(solution)/shard_map/ppermute | solution.py:156
  209.3 21.8 %copy-start.17 = (bf16[512,512]{1,0:T(8,128)(2,1)}, bf16[512,512]{1,0:T(8,128)(2,1)S(1)}, u32[]{:S(2)}) copy-start(bf16[512,512]{1,0:T(8,128)(2,1)S(1)} %collective-permute-done.29.refs_9_) | copy-start | bytes 1572868
  209.3 21.8 %copy-start.18 = (bf16[512,512]{1,0:T(8,128)(2,1)}, bf16[512,512]{1,0:T(8,128)(2,1)S(1)}, u32[]{:S(2)}) copy-start(bf16[512,512]{1,0:T(8,128)(2,1)S(1)} %collective-permute-done.30.refs_10_) | copy-start | bytes 1572868
  210.3 43.4 %collective-permute-start.31 = (bf16[1024,512]{1,0:T(8,128)(2,1)}, bf16[1024,512]{1,0:T(8,128)(2,1)}, u32[]{:S(2)}, u32[]{:S(2)}) collective-permute-start(bf16[1024,512]{1,0:T(8,128)(2,1)} %pad_maximum_fusion.2), channel_id=1, source_target_pairs={{0,4},{1,5},{2,6},{3,7},{4,0},{5,1},{6,2},{7,3},{8,12},{9,13},{10,... | collective-permute-start | bytes 3145736 | tf_op jit(solution)/shard_map/ppermute | solution.py:156
  219.9 33.8 %collective-permute-start.27 = (bf16[2,384,512]{2,1,0:T(8,128)(2,1)S(1)}, bf16[2,384,512]{2,1,0:T(8,128)(2,1)S(1)}, u32[]{:S(2)}, u32[]{:S(2)}) collective-permute-start(bf16[2,384,512]{2,1,0:T(8,128)(2,1)S(1)} %copy-done.27), channel_id=1, source_target_pairs={{0,2},{1,3},{2,0},{3,1},{4,6},{5,7},{6,4},{7,5},{8,10},{9,11},{10,... | collective-permute-start | bytes 2359304 | tf_op jit(solution)/shard_map/ppermute | solution.py:156
  253.7 18.2 %collective-permute-start.32 = (bf16[2,384,512]{2,1,0:T(8,128)(2,1)}, bf16[2,384,512]{2,1,0:T(8,128)(2,1)S(1)}, u32[]{:S(2)}, u32[]{:S(2)}) collective-permute-start(bf16[2,384,512]{2,1,0:T(8,128)(2,1)} %attend.5), channel_id=1, source_target_pairs={{0,2},{1,3},{2,0},{3,1},{4,6},{5,7},{6,4},{7,5},{8,10},{9,11},{10,... | collective-permute-start | bytes 2359304 | tf_op jit(solution)/shard_map/ppermute | solution.py:156
  253.7 41.4 %copy-start.21 = (bf16[2,384,512]{2,1,0:T(8,128)(2,1)}, bf16[2,384,512]{2,1,0:T(8,128)(2,1)S(1)}, u32[]{:S(2)}) copy-start(bf16[2,384,512]{2,1,0:T(8,128)(2,1)S(1)} %collective-permute-done.27.refs_1_) | copy-start | bytes 2359300
  268.1 27.0 %copy-start.5 = (bf16[2,384,512]{2,1,0:T(8,128)(2,1)S(1)}, bf16[2,384,512]{2,1,0:T(8,128)(2,1)}, u32[]{:S(2)}) copy-start(bf16[2,384,512]{2,1,0:T(8,128)(2,1)} %get-tuple-element.127.query_ref.refs_0_) | copy-start | bytes 2359300
  268.1 20.6 %collective-permute-start.33 = (bf16[2,384,512]{2,1,0:T(8,128)(2,1)}, bf16[2,384,512]{2,1,0:T(8,128)(2,1)S(1)}, u32[]{:S(2)}, u32[]{:S(2)}) collective-permute-start(bf16[2,384,512]{2,1,0:T(8,128)(2,1)} %get-tuple-element.152.query_ref), channel_id=1, source_target_pairs={{0,2},{1,3},{2,0},{3,1},{4,6},{5,7},{6,4},{7,5},{8,10},{9,11},{10,... | collective-permute-start | bytes 2359304 | tf_op jit(solution)/shard_map/ppermute | solution.py:156
  271.9 50.0 %copy-start.22 = (bf16[2,384,512]{2,1,0:T(8,128)(2,1)}, bf16[2,384,512]{2,1,0:T(8,128)(2,1)S(1)}, u32[]{:S(2)}) copy-start(bf16[2,384,512]{2,1,0:T(8,128)(2,1)S(1)} %collective-permute-done.32.refs_9_) | copy-start | bytes 2359300
  288.7 35.0 %copy-start.23 = (bf16[2,384,512]{2,1,0:T(8,128)(2,1)}, bf16[2,384,512]{2,1,0:T(8,128)(2,1)S(1)}, u32[]{:S(2)}) copy-start(bf16[2,384,512]{2,1,0:T(8,128)(2,1)S(1)} %collective-permute-done.33.refs_5_) | copy-start | bytes 2359300
  288.7 36.5 %collective-permute-start.36 = (bf16[2,384,512]{2,1,0:T(8,128)(2,1)}, bf16[2,384,512]{2,1,0:T(8,128)(2,1)}, u32[]{:S(2)}, u32[]{:S(2)}) collective-permute-start(bf16[2,384,512]{2,1,0:T(8,128)(2,1)} %attend.6), channel_id=1, source_target_pairs={{0,2},{1,3},{2,0},{3,1},{4,6},{5,7},{6,4},{7,5},{8,10},{9,11},{10,... | collective-permute-start | bytes 2359304 | tf_op jit(solution)/shard_map/ppermute | solution.py:156
  296.1 31.8 %collective-permute-start.28 = (bf16[2,384,512]{2,1,0:T(8,128)(2,1)}, bf16[2,384,512]{2,1,0:T(8,128)(2,1)S(1)}, u32[]{:S(2)}, u32[]{:S(2)}) collective-permute-start(bf16[2,384,512]{2,1,0:T(8,128)(2,1)} %pad_maximum_fusion.6), channel_id=1, source_target_pairs={{0,1},{1,0},{2,3},{3,2},{4,5},{5,4},{6,7},{7,6},{8,9},{9,8},{10,11... | collective-permute-start | bytes 2359304 | tf_op jit(solution)/shard_map/ppermute | solution.py:156
  299.1 22.7 %copy-start.6 = (bf16[2,384,512]{2,1,0:T(8,128)(2,1)S(1)}, bf16[2,384,512]{2,1,0:T(8,128)(2,1)}, u32[]{:S(2)}) copy-start(bf16[2,384,512]{2,1,0:T(8,128)(2,1)} %get-tuple-element.149.query_ref.refs_4_) | copy-start | bytes 2359300
  323.8 4.2 %collective-permute-start.35 = (bf16[2,384,512]{2,1,0:T(8,128)(2,1)}, bf16[2,384,512]{2,1,0:T(8,128)(2,1)S(1)}, u32[]{:S(2)}, u32[]{:S(2)}) collective-permute-start(bf16[2,384,512]{2,1,0:T(8,128)(2,1)} %pad_maximum_fusion.8), channel_id=1, source_target_pairs={{0,1},{1,0},{2,3},{3,2},{4,5},{5,4},{6,7},{7,6},{8,9},{9,8},{10,11... | collective-permute-start | bytes 2359304 | tf_op jit(solution)/shard_map/ppermute | solution.py:156
  324.7 3.2 collective-permute-start.34
  327.2 2.5 collective-permute-start.37
  (44 other events, 177.9 us)
